TPU v7x, 256 devices: a whole 4x4x8 slice. The times are simulated.
256 devices in a mesh: seq: 32 (over x_hi, z, core), ch: 8 (over y, x_lo).
Axes of the slice: x: 4 (x_hi: 2, x_lo: 2; x = x_hi * 2 + x_lo), y: 4, z: 8, core: 2. Of those that a mesh axis runs over, the one named last changes fastest.
Arguments:
- query_proj: bfloat16 [4096, 4096], P('seq', 'ch'), may hold values from -6 to 6
- key_proj: bfloat16 [4096, 4096], P('seq', 'ch'), may hold values from -6 to 6
- value_proj: bfloat16 [4096, 4096], P('seq', 'ch'), may hold values from -6 to 6
- filter_raw: float32 [4096, 4096], P('seq', 'ch'), may hold values from -6 to 6
- rates: float32 [4096], P('ch'), may hold values from 0.5 to 60
- out_weight: bfloat16 [4096, 4096], P('ch', 'seq'), may hold values from -0.09375 to 0.09375
- cotangent: bfloat16 [4096, 4096], P('seq', 'ch'), may hold values from -6 to 6
Outputs:
- grad_query: bfloat16 [4096, 4096], P('seq', 'ch')
- grad_key: bfloat16 [4096, 4096], P('seq', 'ch')
- grad_value: bfloat16 [4096, 4096], P('seq', 'ch')
- grad_filter: float32 [4096, 4096], P('seq', 'ch')
- grad_weight: float32 [4096, 4096], P('ch', 'seq')
All inputs are finite; a program needn't handle non-finite values.
Results may differ from a plain program's by a relative error of at most 0.0029.
Values may be sent and summed in bfloat16 or wider, within the bound.
A program may use at most 64 MiB of HBM per device.

v0:
```python
import jax
import jax.numpy as jnp
from jax import lax
from jax.sharding import PartitionSpec as P

HIGHEST = lax.Precision.HIGHEST
TWO_PI = 6.283185307179586


def phase_table(left, right, period):
    turns = left[:, None] * right[None, :] % period
    signed = jnp.where(2 * turns >= period, turns - period, turns)
    angle = signed.astype(jnp.float32) * (TWO_PI / period)
    return (jnp.cos(angle), jnp.sin(angle))


def spectral_tables(rows):
    parts = lax.axis_size("seq")
    group = rows // parts
    padded = 2 * parts * rows
    here = lax.axis_index("seq")
    blocks = jnp.arange(parts, dtype=jnp.int32)
    slots = jnp.arange(2 * parts, dtype=jnp.int32)
    owner = slots // 2
    freqs = jnp.where(slots % 2 == 0, owner, jnp.where(owner == 0, parts, 2 * parts - owner))
    outer_cos, outer_sin = phase_table(freqs, blocks, 2 * parts)
    samples = here * group + jnp.arange(group, dtype=jnp.int32)
    twist_cos, twist_sin = phase_table(freqs, samples, padded)
    inner = jnp.arange(rows, dtype=jnp.int32)
    inner_cos, inner_sin = phase_table(inner, inner, rows)
    return (
        outer_cos,
        outer_sin,
        twist_cos[None, :, :, None],
        twist_sin[None, :, :, None],
        inner_cos,
        inner_sin,
    )


def forward_spectrum(signal, tables):
    outer_cos, outer_sin, twist_cos, twist_sin, inner_cos, inner_sin = tables
    count, rows, chans = signal.shape
    parts = lax.axis_size("seq")
    group = rows // parts
    pieces = signal.reshape(count, parts, group, chans)
    moved = lax.all_to_all(pieces, "seq", split_axis=1, concat_axis=1, tiled=True)
    real_part = jnp.einsum("kp,mpjc->mkjc", outer_cos, moved, precision=HIGHEST)
    imag_part = -jnp.einsum("kp,mpjc->mkjc", outer_sin, moved, precision=HIGHEST)
    turned_real = real_part * twist_cos + imag_part * twist_sin
    turned_imag = imag_part * twist_cos - real_part * twist_sin
    stacked = jnp.stack([turned_real, turned_imag], axis=1)
    spread = lax.all_to_all(stacked, "seq", split_axis=2, concat_axis=3, tiled=True)
    spread_real = spread[:, 0]
    spread_imag = spread[:, 1]
    out_real = jnp.einsum("ks,masc->makc", inner_cos, spread_real, precision=HIGHEST) + jnp.einsum(
        "ks,masc->makc", inner_sin, spread_imag, precision=HIGHEST
    )
    out_imag = jnp.einsum("ks,masc->makc", inner_cos, spread_imag, precision=HIGHEST) - jnp.einsum(
        "ks,masc->makc", inner_sin, spread_real, precision=HIGHEST
    )
    return (out_real, out_imag)


def inverse_spectrum(spec_real, spec_imag, tables):
    outer_cos, outer_sin, twist_cos, twist_sin, inner_cos, inner_sin = tables
    count, slot_pair, rows, chans = spec_real.shape
    parts = lax.axis_size("seq")
    group = rows // parts
    padded = 2 * parts * rows
    back_real = jnp.einsum("ks,makc->masc", inner_cos, spec_real, precision=HIGHEST) - jnp.einsum(
        "ks,makc->masc", inner_sin, spec_imag, precision=HIGHEST
    )
    back_imag = jnp.einsum("ks,makc->masc", inner_cos, spec_imag, precision=HIGHEST) + jnp.einsum(
        "ks,makc->masc", inner_sin, spec_real, precision=HIGHEST
    )
    stacked = jnp.stack([back_real, back_imag], axis=1).reshape(
        count, 2, slot_pair, parts, group, chans
    )
    joined = lax.all_to_all(stacked, "seq", split_axis=3, concat_axis=2, tiled=True)
    joined = joined.reshape(count, 2, 2 * parts, group, chans)
    joined_real = joined[:, 0]
    joined_imag = joined[:, 1]
    turned_real = joined_real * twist_cos - joined_imag * twist_sin
    turned_imag = joined_imag * twist_cos + joined_real * twist_sin
    signal = (
        jnp.einsum("kp,mkjc->mpjc", outer_cos, turned_real, precision=HIGHEST)
        - jnp.einsum("kp,mkjc->mpjc", outer_sin, turned_imag, precision=HIGHEST)
    ) / padded
    homed = lax.all_to_all(signal, "seq", split_axis=1, concat_axis=2, tiled=True)
    return homed.reshape(signal.shape[0], rows, chans)


def on_device(query_proj, key_proj, value_proj, filter_raw, rates, out_weight, cotangent):
    rows, chans = query_proj.shape
    parts = lax.axis_size("seq")
    total = rows * parts
    offset = lax.axis_index("seq") * rows
    positions = (offset + jnp.arange(rows, dtype=jnp.int32)).astype(jnp.float32) / total
    scaling = jnp.sqrt(2.0 * rates / (total * (1.0 - jnp.exp(-2.0 * rates))))
    envelope = jnp.exp(-positions[:, None] * rates[None, :]) * scaling[None, :]
    tables = spectral_tables(rows)
    query_wide = query_proj.astype(jnp.float32)
    key_wide = key_proj.astype(jnp.float32)
    value_wide = value_proj.astype(jnp.float32)
    product = key_wide * value_wide
    filt = filter_raw * envelope
    prod_real, prod_imag = forward_spectrum(product[None], tables)
    filt_real, filt_imag = forward_spectrum(filt[None], tables)
    prod_real, prod_imag = (prod_real[0], prod_imag[0])
    filt_real, filt_imag = (filt_real[0], filt_imag[0])
    wide_grad = lax.all_gather(cotangent, "ch", axis=1, tiled=True)
    columns = wide_grad
    grad_gated = lax.dot_general(
        columns,
        lax.all_gather(out_weight, "seq", axis=1, tiled=True),
        (((1,), (1,)), ((), ())),
        preferred_element_type=jnp.float32,
    )
    grad_mixed = query_wide * grad_gated
    mixed_real = prod_real * filt_real - prod_imag * filt_imag
    mixed_imag = prod_real * filt_imag + prod_imag * filt_real
    mixed = inverse_spectrum(mixed_real[None], mixed_imag[None], tables)[0]
    grad_real, grad_imag = forward_spectrum(grad_mixed[None], tables)
    grad_real = grad_real[0]
    grad_imag = grad_imag[0]
    back_real = grad_real * filt_real + grad_imag * filt_imag
    back_imag = grad_imag * filt_real - grad_real * filt_imag
    taps_real = grad_real * prod_real + grad_imag * prod_imag
    taps_imag = grad_imag * prod_real - grad_real * prod_imag
    grad_product = inverse_spectrum(back_real[None], back_imag[None], tables)[0]
    grad_taps = inverse_spectrum(taps_real[None], taps_imag[None], tables)[0]
    gated = (query_wide * mixed).astype(jnp.bfloat16)
    grad_query = (mixed * grad_gated).astype(jnp.bfloat16)
    grad_key = (grad_product * value_wide).astype(jnp.bfloat16)
    grad_value = (grad_product * key_wide).astype(jnp.bfloat16)
    grad_filter = grad_taps * envelope
    columns = wide_grad
    owned = lax.psum_scatter(
        lax.dot_general(
            columns, gated, (((0,), (0,)), ((), ())), preferred_element_type=jnp.float32
        ),
        "seq",
        scatter_dimension=0,
        tiled=True,
    )
    grad_weight = owned.T
    return (grad_query, grad_key, grad_value, grad_filter, grad_weight)


def solution(mesh):
    return jax.shard_map(
        on_device,
        mesh=mesh,
        in_specs=(
            P("seq", "ch"),
            P("seq", "ch"),
            P("seq", "ch"),
            P("seq", "ch"),
            P("ch"),
            P("ch", "seq"),
            P("seq", "ch"),
        ),
        out_specs=(P("seq", "ch"), P("seq", "ch"), P("seq", "ch"), P("seq", "ch"), P("ch", "seq")),
        check_vma=False,
    )
```

profile of v0, /device:TPU:8, one launch (start us, length us, event | category | flops | bytes accessed | tf_op | source)
XLA Modules:
  0.0 582.5 jit_solution(11249603402634608507)
XLA Ops:
  9.4 1.1 fusion.70
  11.2 11.3 %all-to-all-start.2 = ((f32[1,32,4,512]{3,2,0,1:T(4,128)}), f32[1,32,4,512]{3,2,0,1:T(4,128)S(1)}, u32[]{:S(2)}, u32[]{:S(2)}) async-start(f32[1,32,4,512]{3,2,0,1:T(4,128)} %bitcast.20), calls=%async_computation.2 | async-start | bytes 524288 | tf_op jit(solution)/shard_map/all_to_all | solution.py:47
  24.3 13.0 %all-to-all-done.2 = f32[1,32,4,512]{3,2,0,1:T(4,128)S(1)} async-done(((f32[1,32,4,512]{3,2,0,1:T(4,128)}), f32[1,32,4,512]{3,2,0,1:T(4,128)S(1)}, u32[]{:S(2)}, u32[]{:S(2)}) %all-to-all-start.2) | async-done | bytes 262176 | tf_op jit(solution)/shard_map/all_to_all | solution.py:47
  37.3 3.9 all-to-all-start
  41.2 14.1 %all-gather.3.cloned.1.call-done = bf16[128,4096]{1,0:T(8,128)(2,1)} async-done(((bf16[128,512]{1,0:T(8,128)(2,1)}), bf16[128,4096]{1,0:T(8,128)(2,1)}) %all-gather.3.cloned.1.call-update) | async-done | bytes 1048592 | tf_op jit(solution)/shard_map/all_gather | solution.py:112
  55.3 91.9 %all-gather.5.cloned.1.call-done = bf16[512,4096]{1,0:T(8,128)(2,1)} async-done(((bf16[512,128]{1,0:T(8,128)(2,1)}), bf16[512,4096]{1,0:T(8,128)(2,1)}) %all-gather.5.cloned.1.call-update) | async-done | bytes 4194320 | tf_op jit(solution)/shard_map/all_gather | solution.py:116
  147.2 4.0 convert_multiply_fusion.1
  152.0 4.7 all-to-all-start.6
  159.0 12.4 %all-to-all-done.6 = f32[1,32,4,512]{3,2,0,1:T(4,128)S(1)} async-done(((f32[1,32,4,512]{3,2,0,1:T(4,128)}), f32[1,32,4,512]{3,2,0,1:T(4,128)S(1)}, u32[]{:S(2)}, u32[]{:S(2)}) %all-to-all-start.6) | async-done | bytes 262176 | tf_op jit(solution)/shard_map/all_to_all | solution.py:47
  172.9 2.0 add_bitcast_fusion
  174.9 1.7 copy.170
  176.6 4.1 all-to-all-start.7
  180.8 1.7 copy.146
  182.4 28.1 %all-to-all-done.7 = f32[1,2,64,4,512]{4,3,1,0,2:T(4,128)S(1)} async-done(((f32[1,2,64,4,512]{4,3,1,0,2:T(4,128)}), f32[1,2,64,4,512]{4,3,1,0,2:T(4,128)S(1)}, u32[]{:S(2)}, u32[]{:S(2)}) %all-to-all-start.7) | async-done | bytes 1048608 | tf_op jit(solution)/shard_map/all_to_all | solution.py:53
  210.5 4.1 all-to-all-start.3
  214.7 1.7 copy.138
  218.0 26.5 %all-to-all-done.3 = f32[1,2,64,4,512]{4,3,1,0,2:T(4,128)S(1)} async-done(((f32[1,2,64,4,512]{4,3,1,0,2:T(4,128)}), f32[1,2,64,4,512]{4,3,1,0,2:T(4,128)S(1)}, u32[]{:S(2)}, u32[]{:S(2)}) %all-to-all-start.3) | async-done | bytes 1048608 | tf_op jit(solution)/shard_map/all_to_all | solution.py:53
  245.5 4.2 all-to-all-start.1
  249.8 2.0 copy.147
  251.8 1.2 fusion.389
  253.2 1.2 copy.239
  255.3 1.7 fusion.27
  258.6 1.6 convolution_add_fusion.2
  260.3 1.6 convolution_add_fusion.4
  261.9 1.6 convolution_subtract_fusion.4
  263.5 16.0 %all-to-all-done.1 = f32[1,2,64,4,512]{4,3,1,0,2:T(4,128)S(1)} async-done(((f32[1,2,64,4,512]{4,3,1,0,2:T(4,128)}), f32[1,2,64,4,512]{4,3,1,0,2:T(4,128)S(1)}, u32[]{:S(2)}, u32[]{:S(2)}) %all-to-all-start.1) | async-done | bytes 1048608 | tf_op jit(solution)/shard_map/all_to_all | solution.py:53
  283.6 1.1 convolution_add_fusion.5
  284.7 2.5 multiply_add_fusion.1
  291.9 1.3 pad_maximum_fusion.5
  293.2 1.1 copy.236
  294.4 4.7 all-to-all-start.10
  303.2 1.1 copy.230
  304.3 24.6 %all-to-all-done.10 = f32[1,2,2,32,4,512]{5,4,2,1,0,3:T(4,128)} async-done(((f32[1,2,2,32,4,512]{5,4,2,1,0,3:T(4,128)}), f32[1,2,2,32,4,512]{5,4,2,1,0,3:T(4,128)}, u32[]{:S(2)}, u32[]{:S(2)}) %all-to-all-start.10) | async-done | bytes 1048608 | tf_op jit(solution)/shard_map/all_to_all | solution.py:80
  328.9 4.3 all-to-all-start.4
  337.4 1.1 copy.235
  338.5 24.6 %all-to-all-done.4 = f32[1,2,2,32,4,512]{5,4,2,1,0,3:T(4,128)S(1)} async-done(((f32[1,2,2,32,4,512]{5,4,2,1,0,3:T(4,128)}), f32[1,2,2,32,4,512]{5,4,2,1,0,3:T(4,128)S(1)}, u32[]{:S(2)}, u32[]{:S(2)}) %all-to-all-start.4) | async-done | bytes 1048608 | tf_op jit(solution)/shard_map/all_to_all | solution.py:80
  363.1 4.7 all-to-all-start.8
  369.2 1.3 copy.194
  370.6 27.0 %all-to-all-done.8 = f32[1,2,2,32,4,512]{5,4,2,1,0,3:T(4,128)} async-done(((f32[1,2,2,32,4,512]{5,4,2,1,0,3:T(4,128)}), f32[1,2,2,32,4,512]{5,4,2,1,0,3:T(4,128)}, u32[]{:S(2)}, u32[]{:S(2)}) %all-to-all-start.8) | async-done | bytes 1048608 | tf_op jit(solution)/shard_map/all_to_all | solution.py:80
  397.6 1.3 copy.184
  398.9 3.0 multiply_add_fusion
  403.3 18.6 %all_to_all.141 = f32[1,32,4,512]{3,2,0,1:T(4,128)S(1)} all-to-all(f32[1,32,4,512]{3,2,0,1:T(4,128)S(1)} %copy.167), channel_id=1, replica_groups=mesh['seq'=32,'ch'=8] {'seq'}, dimensions={1} | all-to-all | bytes 524288 | tf_op jit(solution)/shard_map/all_to_all | solution.py:90
  422.0 4.6 convolution_bitcast_fusion
  429.7 3.9 all-to-all-start.11
  435.7 12.6 %all-to-all-done.11 = f32[1,32,4,512]{3,2,0,1:T(4,128)S(1)} async-done(((f32[1,32,4,512]{3,2,0,1:T(4,128)}), f32[1,32,4,512]{3,2,0,1:T(4,128)S(1)}, u32[]{:S(2)}, u32[]{:S(2)}) %all-to-all-start.11) | async-done | bytes 262176 | tf_op jit(solution)/shard_map/all_to_all | solution.py:90
  448.2 3.9 all-to-all-start.9
  452.2 14.6 %all-to-all-done.9 = f32[1,32,4,512]{3,2,0,1:T(4,128)S(1)} async-done(((f32[1,32,4,512]{3,2,0,1:T(4,128)}), f32[1,32,4,512]{3,2,0,1:T(4,128)S(1)}, u32[]{:S(2)}, u32[]{:S(2)}) %all-to-all-start.9) | async-done | bytes 262176 | tf_op jit(solution)/shard_map/all_to_all | solution.py:90
  469.2 106.4 %reduce-scatter.2.cloned.1.call-done = f32[128,512]{0,1:T(8,128)} async-done(((f32[4096,512]{0,1:T(8,128)}), f32[128,512]{0,1:T(8,128)}) %reduce-scatter.2.cloned.1.call-update) | async-done | bytes 262160 | tf_op jit(solution)/shard_map/reduce_scatter | solution.py:139
  (105 shorter events, 42.3 us)
Async XLA Ops:
  7.2 48.2 %all-gather.3.cloned.1.call-start = ((), (), s32[]{:S(2)}) async-start(), calls=%async_computation.13 | async-start | bytes 1179648 | tf_op jit(solution)/shard_map/all_gather | solution.py:112
  7.9 139.3 %all-gather.5.cloned.1.call-start = ((), (), s32[]{:S(2)}) async-start(), calls=%async_computation.14 | async-start | bytes 4325376 | tf_op jit(solution)/shard_map/all_gather | solution.py:116
  11.2 26.1 %all-to-all-start.2 = ((f32[1,32,4,512]{3,2,0,1:T(4,128)}), f32[1,32,4,512]{3,2,0,1:T(4,128)S(1)}, u32[]{:S(2)}, u32[]{:S(2)}) async-start(f32[1,32,4,512]{3,2,0,1:T(4,128)} %bitcast.20), calls=%async_computation.2 | async-start | bytes 524288 | tf_op jit(solution)/shard_map/all_to_all | solution.py:47
  37.3 114.7 %all-to-all-start = ((f32[1,32,4,512]{3,2,0,1:T(4,128)}), f32[1,32,4,512]{3,2,0,1:T(4,128)S(1)}, u32[]{:S(2)}, u32[]{:S(2)}) async-start(f32[1,32,4,512]{3,2,0,1:T(4,128)} %bitcast), calls=%async_computation | async-start | bytes 524288 | tf_op jit(solution)/shard_map/all_to_all | solution.py:47
  152.0 19.4 %all-to-all-start.6 = ((f32[1,32,4,512]{3,2,0,1:T(4,128)}), f32[1,32,4,512]{3,2,0,1:T(4,128)S(1)}, u32[]{:S(2)}, u32[]{:S(2)}) async-start(f32[1,32,4,512]{3,2,0,1:T(4,128)} %bitcast.65), calls=%async_computation.6 | async-start | bytes 524288 | tf_op jit(solution)/shard_map/all_to_all | solution.py:47
  174.8 5.9 %copy-start.8 = (f32[1,1,64,4,512]{4,2,3,1,0:T(8,128)S(1)}, f32[1,1,64,4,512]{4,2,3,1,0:T(8,128)}, u32[]{:S(2)}) copy-start(f32[1,1,64,4,512]{4,2,3,1,0:T(8,128)} %get-tuple-element.39) | copy-start | bytes 1572868
  174.8 5.9 %copy-start.9 = (f32[1,1,64,4,512]{4,2,3,1,0:T(8,128)S(1)}, f32[1,1,64,4,512]{4,2,3,1,0:T(8,128)}, u32[]{:S(2)}) copy-start(f32[1,1,64,4,512]{4,2,3,1,0:T(8,128)} %get-tuple-element.40) | copy-start | bytes 1572868
  176.6 38.0 %copy-start.7 = (f32[1,1,64,4,512]{4,2,3,1,0:T(8,128)S(1)}, f32[1,1,64,4,512]{4,2,3,1,0:T(8,128)}, u32[]{:S(2)}) copy-start(f32[1,1,64,4,512]{4,2,3,1,0:T(8,128)} %get-tuple-element.42) | copy-start | bytes 1572868
  176.6 33.9 %all-to-all-start.7 = ((f32[1,2,64,4,512]{4,3,1,0,2:T(4,128)}), f32[1,2,64,4,512]{4,3,1,0,2:T(4,128)S(1)}, u32[]{:S(2)}, u32[]{:S(2)}) async-start(f32[1,2,64,4,512]{4,3,1,0,2:T(4,128)} %copy.170), calls=%async_computation.7 | async-start | bytes 2097152 | tf_op jit(solution)/shard_map/all_to_all | solution.py:53
  210.5 34.0 %all-to-all-start.3 = ((f32[1,2,64,4,512]{4,3,1,0,2:T(4,128)}), f32[1,2,64,4,512]{4,3,1,0,2:T(4,128)S(1)}, u32[]{:S(2)}, u32[]{:S(2)}) async-start(f32[1,2,64,4,512]{4,3,1,0,2:T(4,128)} %copy.146), calls=%async_computation.3 | async-start | bytes 2097152 | tf_op jit(solution)/shard_map/all_to_all | solution.py:53
  244.5 1.0 copy-start.1
  245.5 34.0 %all-to-all-start.1 = ((f32[1,2,64,4,512]{4,3,1,0,2:T(4,128)}), f32[1,2,64,4,512]{4,3,1,0,2:T(4,128)S(1)}, u32[]{:S(2)}, u32[]{:S(2)}) async-start(f32[1,2,64,4,512]{4,3,1,0,2:T(4,128)} %copy.138), calls=%async_computation.1 | async-start | bytes 2097152 | tf_op jit(solution)/shard_map/all_to_all | solution.py:53
  280.6 4.1 copy-start.6
  294.4 34.5 %all-to-all-start.10 = ((f32[1,2,2,32,4,512]{5,4,2,1,0,3:T(4,128)}), f32[1,2,2,32,4,512]{5,4,2,1,0,3:T(4,128)}, u32[]{:S(2)}, u32[]{:S(2)}) async-start(f32[1,2,2,32,4,512]{5,4,2,1,0,3:T(4,128)} %copy.236), calls=%async_computation.10 | async-start | bytes 2097152 | tf_op jit(solution)/shard_map/all_to_all | solution.py:80
  328.9 34.2 %all-to-all-start.4 = ((f32[1,2,2,32,4,512]{5,4,2,1,0,3:T(4,128)}), f32[1,2,2,32,4,512]{5,4,2,1,0,3:T(4,128)S(1)}, u32[]{:S(2)}, u32[]{:S(2)}) async-start(f32[1,2,2,32,4,512]{5,4,2,1,0,3:T(4,128)} %copy.230), calls=%async_computation.4 | async-start | bytes 2097152 | tf_op jit(solution)/shard_map/all_to_all | solution.py:80
  363.1 34.5 %all-to-all-start.8 = ((f32[1,2,2,32,4,512]{5,4,2,1,0,3:T(4,128)}), f32[1,2,2,32,4,512]{5,4,2,1,0,3:T(4,128)}, u32[]{:S(2)}, u32[]{:S(2)}) async-start(f32[1,2,2,32,4,512]{5,4,2,1,0,3:T(4,128)} %copy.235), calls=%async_computation.8 | async-start | bytes 2097152 | tf_op jit(solution)/shard_map/all_to_all | solution.py:80
  367.8 207.8 %reduce-scatter.2.cloned.1.call-start = ((), (), s32[]{:S(2)}) async-start(), calls=%async_computation.15 | async-start | bytes 8650752 | tf_op jit(solution)/shard_map/reduce_scatter | solution.py:139
  398.9 23.1 %copy-start = (bf16[128,4096]{1,0:T(8,128)(2,1)S(1)}, bf16[128,4096]{1,0:T(8,128)(2,1)}, u32[]{:S(2)}) copy-start(bf16[128,4096]{1,0:T(8,128)(2,1)} %all-gather.3.cloned.1.call-done) | copy-start | bytes 3145732
  398.9 23.1 %copy-start.10 = (bf16[128,512]{1,0:T(8,128)(2,1)S(1)}, bf16[128,512]{1,0:T(8,128)(2,1)}, u32[]{:S(2)}) copy-start(bf16[128,512]{1,0:T(8,128)(2,1)} %param.7) | copy-start | bytes 393220
  426.6 1.0 copy-start.3
  426.6 1.6 copy-start.5
  426.6 7.0 %copy-start.2 = (f32[64,4,512]{2,1,0:T(4,128)S(1)}, f32[64,4,512]{2,1,0:T(4,128)}, u32[]{:S(2)}) copy-start(f32[64,4,512]{2,1,0:T(4,128)} %get-tuple-element.37) | copy-start | bytes 1572868
  426.6 7.6 %copy-start.4 = (f32[64,4,512]{2,1,0:T(4,128)S(1)}, f32[64,4,512]{2,1,0:T(4,128)}, u32[]{:S(2)}) copy-start(f32[64,4,512]{2,1,0:T(4,128)} %get-tuple-element.38) | copy-start | bytes 1572868
  426.6 40.3 %copy-start.13 = (f32[512]{0:T(512)S(1)}, f32[512]{0:T(512)}, u32[]{:S(2)}) copy-start(f32[512]{0:T(512)} %param.11) | copy-start | bytes 6148
  426.6 41.8 %copy-start.11 = (bf16[128,512]{1,0:T(8,128)(2,1)S(1)}, bf16[128,512]{1,0:T(8,128)(2,1)}, u32[]{:S(2)}) copy-start(bf16[128,512]{1,0:T(8,128)(2,1)} %param.9) | copy-start | bytes 393220
  426.6 41.8 %copy-start.12 = (bf16[128,512]{1,0:T(8,128)(2,1)S(1)}, bf16[128,512]{1,0:T(8,128)(2,1)}, u32[]{:S(2)}) copy-start(bf16[128,512]{1,0:T(8,128)(2,1)} %param.8) | copy-start | bytes 393220
  429.7 18.6 %all-to-all-start.11 = ((f32[1,32,4,512]{3,2,0,1:T(4,128)}), f32[1,32,4,512]{3,2,0,1:T(4,128)S(1)}, u32[]{:S(2)}, u32[]{:S(2)}) async-start(f32[1,32,4,512]{3,2,0,1:T(4,128)} %copy.197), calls=%async_computation.11 | async-start | bytes 524288 | tf_op jit(solution)/shard_map/all_to_all | solution.py:90
  448.2 18.6 %all-to-all-start.9 = ((f32[1,32,4,512]{3,2,0,1:T(4,128)}), f32[1,32,4,512]{3,2,0,1:T(4,128)S(1)}, u32[]{:S(2)}, u32[]{:S(2)}) async-start(f32[1,32,4,512]{3,2,0,1:T(4,128)} %copy.187), calls=%async_computation.9 | async-start | bytes 524288 | tf_op jit(solution)/shard_map/all_to_all | solution.py:90
Sparse Core Ops, SparseCore 0:
  9.8 45.4 all-gather.2
  57.9 89.3 all-gather.4
  426.7 148.7 reduce-scatter.1
where the time goes:
time: 593 us; the launch traced here: 583 us
  waiting for transfers between devices  413 us (70%)
  starting transfers between devices  53.8 us (9%)
  matrix products  43.4 us (7%)
  local copies, waits for them, and re-layouts  28.7 us (5%)
  blocking collectives  18.6 us (3%)
  between operations  14.9 us (3%)
  other arithmetic  10.2 us (2%)
    reduce_scatter x1, waiting for transfers between devices, on_device(): lax.psum_scatter(lax.dot_general(columns, gated, (((0,), (0,)), ((), ()))...  106 us
    all_gather x1, waiting for transfers between devices, on_device(): lax.all_gather(out_weight, 'seq', axis=1, tiled=True)  91.9 us
    all_to_all x3, waiting for transfers between devices, inverse_spectrum(): lax.all_to_all(stacked, 'seq', split_axis=3, concat_axis=2, tiled=True)  76.1 us
    all_to_all x3, waiting for transfers between devices, forward_spectrum(): lax.all_to_all(stacked, 'seq', split_axis=2, concat_axis=3, tiled=True)  70.5 us
    all_to_all x2, waiting for transfers between devices, inverse_spectrum(): lax.all_to_all(signal, 'seq', split_axis=1, concat_axis=2, tiled=True)  27.2 us
    all_to_all x3, waiting for transfers between devices, forward_spectrum(): lax.all_to_all(pieces, 'seq', split_axis=1, concat_axis=1, tiled=True)  25.4 us
    all_to_all x3, starting transfers between devices, forward_spectrum(): lax.all_to_all(pieces, 'seq', split_axis=1, concat_axis=1, tiled=True)  19.9 us
    all_to_all x1, blocking collectives, inverse_spectrum(): lax.all_to_all(signal, 'seq', split_axis=1, concat_axis=2, tiled=True)  18.6 us
  transfers between devices with their start and end apart: 14, of which 13 were waited for; matrix products, arithmetic and copies ran while one was open for 9% of the time, Pallas kernels for 0%

commit v1 on v0

v1 whole, which is shorter than its diff:
```python
import math

import jax
import jax.numpy as jnp
import numpy as np
from jax import lax
from jax.sharding import PartitionSpec as P

PREC = lax.Precision.HIGH


def transform_tables(parts, rows):
    total = 2 * parts * rows
    k1 = np.arange(parts + 1)[:, None]
    n1 = np.arange(parts)[None, :]
    turn = 2 * math.pi * ((k1 * n1) % (2 * parts)) / (2 * parts)
    outer = np.concatenate([np.cos(turn), -np.sin(turn)], 0)
    weight = np.full((parts + 1, 1), 2.0)
    weight[0] = weight[-1] = 1.0
    outer_back = np.concatenate([weight * np.cos(turn), -weight * np.sin(turn)], 0).T / total
    n2 = np.arange(rows)
    twist = 2 * math.pi * (k1 * n2[None, :]) / total
    inner = 2 * math.pi * ((n2[:, None] * n2[None, :]) % rows) / rows
    cos, sin = np.cos(inner), np.sin(inner)
    ahead = np.block([[cos, -sin], [sin, cos]])
    back = np.block([[cos, sin], [-sin, cos]])
    return tuple(
        np.asarray(a, np.float32)
        for a in (outer, outer_back, np.cos(twist), np.sin(twist), ahead, back)
    )


def forward(x, tables):
    outer, _, tc, ts, ahead, _ = tables
    parts, c, rows = x.shape
    y = jnp.einsum("kp,pcn->kcn", outer, x, precision=PREC)
    re, im = y[: parts + 1], y[parts + 1 :]
    tc, ts = tc[:, None, :], ts[:, None, :]
    z = jnp.concatenate([re * tc + im * ts, im * tc - re * ts], -1)
    z = jnp.einsum("kcn,nm->kcm", z, ahead, precision=PREC)
    return z[..., :rows], z[..., rows:]


def inverse(re, im, tables):
    _, outer_back, tc, ts, _, back = tables
    rows = re.shape[-1]
    z = jnp.einsum("kcn,nm->kcm", jnp.concatenate([re, im], -1), back, precision=PREC)
    re, im = z[..., :rows], z[..., rows:]
    tc, ts = tc[:, None, :], ts[:, None, :]
    z = jnp.concatenate([re * tc - im * ts, im * tc + re * ts], 0)
    return jnp.einsum("pk,kcn->pcn", outer_back, z, precision=PREC)


def exchange(x):
    return lax.all_to_all(x, "seq", 0, 0, tiled=True)


def on_device(query, key, value, filter_raw, rates, out_weight, cotangent):
    rows, chans = query.shape
    parts = lax.axis_size("seq")
    fine = chans // parts
    total = rows * parts
    tables = transform_tables(parts, rows)
    offset = lax.axis_index("seq") * rows
    positions = (offset + jnp.arange(rows, dtype=jnp.int32)).astype(jnp.float32) / total
    scaling = jnp.sqrt(2.0 * rates / (total * (1.0 - jnp.exp(-2.0 * rates))))
    envelope = jnp.exp(-rates[:, None] * positions[None, :]) * scaling[:, None]

    def spread(x):
        return exchange(x.reshape(parts, fine, rows))

    key_t = key.T.astype(jnp.float32)
    value_t = value.T.astype(jnp.float32)
    query_t = query.T
    product = spread(key_t * value_t)
    filt = spread(filter_raw.T * envelope)
    query_c = spread(query_t)
    wide_cot = lax.all_gather(cotangent, "ch", axis=1, tiled=True)
    wide_weight = lax.all_gather(out_weight, "seq", axis=1, tiled=True)
    grad_gated = lax.dot_general(
        wide_weight, wide_cot, (((1,), (1,)), ((), ())), preferred_element_type=jnp.float32
    )
    grad_mixed = spread(query_t.astype(jnp.float32) * grad_gated)
    tall_cot = exchange(wide_cot.reshape(rows, parts, -1).transpose(1, 0, 2))

    pr, pi = forward(product, tables)
    fr, fi = forward(filt, tables)
    mixed = inverse(pr * fr - pi * fi, pr * fi + pi * fr, tables)
    gated = (query_c.astype(jnp.float32) * mixed).astype(jnp.bfloat16)
    all_gated = lax.all_gather(gated, "seq", axis=0)
    gr, gi = forward(grad_mixed, tables)
    grad_product = inverse(gr * fr + gi * fi, gi * fr - gr * fi, tables)
    grad_taps = inverse(gr * pr + gi * pi, gi * pr - gr * pi, tables)

    def home(x):
        return exchange(x).reshape(chans, rows)

    mixed_h = home(mixed)
    grad_product_h = home(grad_product)
    grad_taps_h = home(grad_taps)
    grad_query = (mixed_h * grad_gated).astype(jnp.bfloat16).T
    grad_key = (grad_product_h * value_t).astype(jnp.bfloat16).T
    grad_value = (grad_product_h * key_t).astype(jnp.bfloat16).T
    grad_filter = (grad_taps_h * envelope).T
    grad_weight = jnp.einsum(
        "sptr,pro->sto", all_gated.transpose(0, 1, 2, 3), tall_cot, preferred_element_type=jnp.float32
    ).reshape(chans, -1)
    return (grad_query, grad_key, grad_value, grad_filter, grad_weight)


def solution(mesh):
    return jax.shard_map(
        on_device,
        mesh=mesh,
        in_specs=(
            P("seq", "ch"),
            P("seq", "ch"),
            P("seq", "ch"),
            P("seq", "ch"),
            P("ch"),
            P("ch", "seq"),
            P("seq", "ch"),
        ),
        out_specs=(P("seq", "ch"), P("seq", "ch"), P("seq", "ch"), P("seq", "ch"), P("ch", "seq")),
        check_vma=False,
    )
```

time: 593 us -> 335 us (0.56)
  the two profiles are of different devices: /device:TPU:8 before, /device:TPU:1 now
where the time goes in v1:
time: 335 us; the launch traced here: 334 us
  waiting for transfers between devices  229 us (68%)
  starting transfers between devices  43.1 us (13%)
  blocking collectives  17.7 us (5%)
  matrix products  16.1 us (5%)
  between operations  14.1 us (4%)
  local copies, waits for them, and re-layouts  11.8 us (4%)
    all_gather x1, waiting for transfers between devices, on_device(): wide_weight = lax.all_gather(out_weight, 'seq', axis=1, tiled=True)  94.3 us
    all_to_all x7, waiting for transfers between devices, exchange(): return lax.all_to_all(x, 'seq', 0, 0, tiled=True)  88.6 us
    all_to_all x7, starting transfers between devices, exchange(): return lax.all_to_all(x, 'seq', 0, 0, tiled=True)  43 us
    all_gather x1, waiting for transfers between devices, on_device(): wide_cot = lax.all_gather(cotangent, 'ch', axis=1, tiled=True)  27.5 us
    all_to_all x1, blocking collectives, exchange(): return lax.all_to_all(x, 'seq', 0, 0, tiled=True)  17.7 us
    all_gather x1, waiting for transfers between devices, on_device(): all_gated = lax.all_gather(gated, 'seq', axis=0)  17.3 us
    unnamed x27, local copies, waits for them, and re-layouts  7.86 us
  transfers between devices with their start and end apart: 10, of which 9 were waited for; matrix products, arithmetic and copies ran while one was open for 6% of the time, Pallas kernels for 0%

profile of v1, /device:TPU:1, one launch (start us, length us, event | category | flops | bytes accessed | tf_op | source)
XLA Modules:
  0.0 334.2 jit_solution(18102318834875755022)
XLA Ops:
  7.2 1.7 copy.86
  9.0 0.7 all-gather.5.cloned.1.call-update
  9.7 1.1 copy.80
  10.8 0.7 fusion.40
  11.5 0.9 bitcast_multiply_fusion.4
  12.4 12.6 %all-to-all-start.1 = ((f32[32,16,128]{2,1,0:T(8,128)}), f32[32,16,128]{2,1,0:T(8,128)S(1)}, u32[]{:S(2)}, u32[]{:S(2)}) async-start(f32[32,16,128]{2,1,0:T(8,128)} %bitcast.7), calls=%async_computation.1 | async-start | bytes 524288 | tf_op jit(solution)/shard_map/all_to_all | solution.py:55
  25.0 1.7 copy.87
  26.7 27.5 %all-gather.7.cloned.1.call-done = bf16[128,4096]{0,1:T(8,128)(2,1)} async-done(((bf16[128,512]{0,1:T(8,128)(2,1)}), bf16[128,4096]{0,1:T(8,128)(2,1)}) %all-gather.7.cloned.1.call-update) | async-done | bytes 1048592 | tf_op jit(solution)/shard_map/all_gather | solution.py:78
  54.2 94.3 %all-gather.5.cloned.1.call-done = bf16[512,4096]{1,0:T(8,128)(2,1)} async-done(((bf16[512,128]{1,0:T(8,128)(2,1)}), bf16[512,4096]{1,0:T(8,128)(2,1)}) %all-gather.5.cloned.1.call-update) | async-done | bytes 4194320 | tf_op jit(solution)/shard_map/all_gather | solution.py:79
  148.6 4.5 %convert_multiply_fusion = (f32[512,128]{1,0:T(8,128)}, f32[512,128]{1,0:T(8,128)S(1)}) fusion(bf16[128,512]{0,1:T(8,128)(2,1)} %copy.87, bf16[512,4096]{1,0:T(8,128)(2,1)} %all-gather.5.cloned.1.call-done, bf16[128,4096]{0,1:T(8,128)(2,1)} %all-gather.7.cloned.1.call-done), kind=kOutput, calls=%fused_computation.67 | convolution fusion | flops 537001984 | bytes 5898240 | tf_op jit(solution)/shard_map/dot_general | solution.py:80
  153.0 4.8 %all-to-all-start.3 = ((f32[32,16,128]{2,1,0:T(8,128)}), f32[32,16,128]{2,1,0:T(8,128)S(1)}, u32[]{:S(2)}, u32[]{:S(2)}) async-start(f32[32,16,128]{2,1,0:T(8,128)} %bitcast.12), calls=%async_computation.3 | async-start | bytes 524288 | tf_op jit(solution)/shard_map/all_to_all | solution.py:55
  157.9 0.4 fusion.32
  158.4 13.0 %all-to-all-done.3 = f32[32,16,128]{2,1,0:T(8,128)S(1)} async-done(((f32[32,16,128]{2,1,0:T(8,128)}), f32[32,16,128]{2,1,0:T(8,128)S(1)}, u32[]{:S(2)}, u32[]{:S(2)}) %all-to-all-start.3) | async-done | bytes 262176 | tf_op jit(solution)/shard_map/all_to_all | solution.py:55
  171.3 0.4 fusion.30
  171.8 0.2 multiply_add_fusion.2
  172.1 0.5 fusion.23
  172.6 0.5 fusion.21
  173.3 0.7 fusion.5
  174.0 0.3 fusion.13
  174.3 0.9 copy.92
  175.2 5.0 %all-to-all-start.4 = ((f32[32,16,128]{2,1,0:T(8,128)}), f32[32,16,128]{2,1,0:T(8,128)S(1)}, u32[]{:S(2)}, u32[]{:S(2)}) async-start(f32[32,16,128]{2,1,0:T(8,128)} %copy.92), calls=%async_computation.4 | async-start | bytes 524288 | tf_op jit(solution)/shard_map/all_to_all | solution.py:55
  180.5 13.3 %all-to-all-done.4 = f32[32,16,128]{2,1,0:T(8,128)S(1)} async-done(((f32[32,16,128]{2,1,0:T(8,128)}), f32[32,16,128]{2,1,0:T(8,128)S(1)}, u32[]{:S(2)}, u32[]{:S(2)}) %all-to-all-start.4) | async-done | bytes 262176 | tf_op jit(solution)/shard_map/all_to_all | solution.py:55
  193.8 17.7 %all_to_all.40 = f32[32,16,128]{2,1,0:T(8,128)S(1)} all-to-all(f32[32,16,128]{2,1,0:T(8,128)S(1)} %bitcast.62), channel_id=1, replica_groups=mesh['seq'=32,'ch'=8] {'seq'}, dimensions={0} | all-to-all | bytes 524288 | tf_op jit(solution)/shard_map/all_to_all | solution.py:55
  211.5 5.0 %all-to-all-start.6 = ((bf16[32,16,128]{2,1,0:T(8,128)(2,1)}), bf16[32,16,128]{2,1,0:T(8,128)(2,1)S(1)}, u32[]{:S(2)}, u32[]{:S(2)}) async-start(bf16[32,16,128]{2,1,0:T(8,128)(2,1)} %bitcast.18), calls=%async_computation.6 | async-start | bytes 262144 | tf_op jit(solution)/shard_map/all_to_all | solution.py:55
  216.6 0.4 fusion.34
  217.2 0.5 fusion.25
  217.9 0.7 fusion.3
  218.6 0.7 fusion.7
  219.3 0.1 multiply_subtract_fusion
  219.4 7.7 %all-to-all-done.6 = bf16[32,16,128]{2,1,0:T(8,128)(2,1)S(1)} async-done(((bf16[32,16,128]{2,1,0:T(8,128)(2,1)}), bf16[32,16,128]{2,1,0:T(8,128)(2,1)S(1)}, u32[]{:S(2)}, u32[]{:S(2)}) %all-to-all-start.6) | async-done | bytes 131104 | tf_op jit(solution)/shard_map/all_to_all | solution.py:55
  227.2 1.0 multiply_convert_fusion
  228.2 0.3 fusion.17
  228.5 0.9 copy.95
  229.3 5.2 %all-to-all-start.5 = ((f32[32,16,128]{2,1,0:T(8,128)}), f32[32,16,128]{2,1,0:T(8,128)S(1)}, u32[]{:S(2)}, u32[]{:S(2)}) async-start(f32[32,16,128]{2,1,0:T(8,128)} %copy.95), calls=%async_computation.5 | async-start | bytes 524288 | tf_op jit(solution)/shard_map/all_to_all | solution.py:55
  234.5 0.9 copy.85
  235.3 13.4 %all-to-all-done.5 = f32[32,16,128]{2,1,0:T(8,128)S(1)} async-done(((f32[32,16,128]{2,1,0:T(8,128)}), f32[32,16,128]{2,1,0:T(8,128)S(1)}, u32[]{:S(2)}, u32[]{:S(2)}) %all-to-all-start.5) | async-done | bytes 262176 | tf_op jit(solution)/shard_map/all_to_all | solution.py:55
  248.8 5.3 %all-to-all-start.2 = ((f32[32,16,128]{2,1,0:T(8,128)}), f32[32,16,128]{2,1,0:T(8,128)S(1)}, u32[]{:S(2)}, u32[]{:S(2)}) async-start(f32[32,16,128]{2,1,0:T(8,128)} %copy.85), calls=%async_computation.2 | async-start | bytes 524288 | tf_op jit(solution)/shard_map/all_to_all | solution.py:55
  254.0 1.4 copy.97
  255.4 12.8 %all-to-all-done.2 = f32[32,16,128]{2,1,0:T(8,128)S(1)} async-done(((f32[32,16,128]{2,1,0:T(8,128)}), f32[32,16,128]{2,1,0:T(8,128)S(1)}, u32[]{:S(2)}, u32[]{:S(2)}) %all-to-all-start.2) | async-done | bytes 262176 | tf_op jit(solution)/shard_map/all_to_all | solution.py:55
  268.2 5.1 %all-to-all-start.7 = ((bf16[32,128,128]{2,1,0:T(8,128)(2,1)}), bf16[32,128,128]{2,1,0:T(8,128)(2,1)S(1)}, u32[]{:S(2)}, u32[]{:S(2)}) async-start(bf16[32,128,128]{2,1,0:T(8,128)(2,1)} %bitcast.21), calls=%async_computation.7 | async-start | bytes 2097152 | tf_op jit(solution)/shard_map/all_to_all | solution.py:55
  273.3 0.8 copy.101
  274.1 0.8 copy.100
  274.9 0.2 bitcast_multiply_fusion
  275.1 0.8 copy.102
  275.9 0.8 copy.99
  276.7 28.4 %all-to-all-done.7 = bf16[32,128,128]{2,1,0:T(8,128)(2,1)S(1)} async-done(((bf16[32,128,128]{2,1,0:T(8,128)(2,1)}), bf16[32,128,128]{2,1,0:T(8,128)(2,1)S(1)}, u32[]{:S(2)}, u32[]{:S(2)}) %all-to-all-start.7) | async-done | bytes 1048608 | tf_op jit(solution)/shard_map/all_to_all | solution.py:55
  305.1 17.3 %all-gather.9.cloned.1.call-done = bf16[1024,16,128]{2,0,1:T(8,128)(2,1)} async-done(((bf16[32,16,128]{2,0,1:T(8,128)(2,1)}), bf16[1024,16,128]{2,0,1:T(8,128)(2,1)}) %all-gather.9.cloned.1.call-update) | async-done | bytes 4194320 | tf_op jit(solution)/shard_map/all_gather | solution.py:90
  322.5 5.3 %fusion = f32[32,16,128,1]{2,1,3,0:T(8,128)} fusion(bf16[32,32,16,128]{3,1,0,2:T(8,128)(2,1)} %bitcast.66, bf16[32,128,128]{2,1,0:T(8,128)(2,1)S(1)} %all-to-all-done.7), kind=kOutput, calls=%fused_computation | convolution fusion | flops 536870912 | bytes 5505024 | tf_op jit(solution)/shard_map/sptr,pro->sto/dot_general | solution.py:105
  (38 shorter events, 1.2 us)
Async XLA Ops:
  7.2 47.1 %all-gather.7.cloned.1.call-start = ((), (), s32[]{:S(2)}) async-start(), calls=%async_computation.9 | async-start | bytes 1179648 | tf_op jit(solution)/shard_map/all_gather | solution.py:78
  8.9 149.0 %copy-start.6 = (f32[66,32,1]{0,1,2:T(8,128)S(1)}, f32[66,32,1]{0,1,2:T(8,128)}, u32[]{:S(2)}) copy-start(f32[66,32,1]{0,1,2:T(8,128)} %constant.40) | copy-start | bytes 25348
  8.9 139.7 %all-gather.5.cloned.1.call-start = ((), (), s32[]{:S(2)}) async-start(), calls=%async_computation.8 | async-start | bytes 4325376 | tf_op jit(solution)/shard_map/all_gather | solution.py:79
  12.4 140.7 %all-to-all-start.1 = ((f32[32,16,128]{2,1,0:T(8,128)}), f32[32,16,128]{2,1,0:T(8,128)S(1)}, u32[]{:S(2)}, u32[]{:S(2)}) async-start(f32[32,16,128]{2,1,0:T(8,128)} %bitcast.7), calls=%async_computation.1 | async-start | bytes 524288 | tf_op jit(solution)/shard_map/all_to_all | solution.py:55
  25.0 146.8 %copy-start.3 = (f32[33,128]{1,0:T(8,128)S(1)}, f32[33,128]{1,0:T(8,128)}, u32[]{:S(2)}) copy-start(f32[33,128]{1,0:T(8,128)} %constant.38) | copy-start | bytes 50692
  25.0 146.8 %copy-start.4 = (f32[33,128]{1,0:T(8,128)S(1)}, f32[33,128]{1,0:T(8,128)}, u32[]{:S(2)}) copy-start(f32[33,128]{1,0:T(8,128)} %constant.37) | copy-start | bytes 50692
  153.0 19.1 %copy-start.2 = (f32[256,256,1]{1,0,2:T(8,128)S(1)}, f32[256,256,1]{1,0,2:T(8,128)}, u32[]{:S(2)}) copy-start(f32[256,256,1]{1,0,2:T(8,128)} %constant.41) | copy-start | bytes 786436
  153.0 18.3 %all-to-all-start.3 = ((f32[32,16,128]{2,1,0:T(8,128)}), f32[32,16,128]{2,1,0:T(8,128)S(1)}, u32[]{:S(2)}, u32[]{:S(2)}) async-start(f32[32,16,128]{2,1,0:T(8,128)} %bitcast.12), calls=%async_computation.3 | async-start | bytes 524288 | tf_op jit(solution)/shard_map/all_to_all | solution.py:55
  172.0 1.3 copy-start.1
  172.1 1.9 copy-start.5
  172.6 7.6 %copy-start.7 = (bf16[128,512]{1,0:T(8,128)(2,1)S(1)}, bf16[128,512]{1,0:T(8,128)(2,1)}, u32[]{:S(2)}) copy-start(bf16[128,512]{1,0:T(8,128)(2,1)} %param.32) | copy-start | bytes 393220
  173.1 7.2 %copy-start.8 = (bf16[128,512]{1,0:T(8,128)(2,1)S(1)}, bf16[128,512]{1,0:T(8,128)(2,1)}, u32[]{:S(2)}) copy-start(bf16[128,512]{1,0:T(8,128)(2,1)} %param.33) | copy-start | bytes 393220
  175.2 18.6 %all-to-all-start.4 = ((f32[32,16,128]{2,1,0:T(8,128)}), f32[32,16,128]{2,1,0:T(8,128)S(1)}, u32[]{:S(2)}, u32[]{:S(2)}) async-start(f32[32,16,128]{2,1,0:T(8,128)} %copy.92), calls=%async_computation.4 | async-start | bytes 524288 | tf_op jit(solution)/shard_map/all_to_all | solution.py:55
  211.5 15.7 %all-to-all-start.6 = ((bf16[32,16,128]{2,1,0:T(8,128)(2,1)}), bf16[32,16,128]{2,1,0:T(8,128)(2,1)S(1)}, u32[]{:S(2)}, u32[]{:S(2)}) async-start(bf16[32,16,128]{2,1,0:T(8,128)(2,1)} %bitcast.18), calls=%async_computation.6 | async-start | bytes 262144 | tf_op jit(solution)/shard_map/all_to_all | solution.py:55
  216.5 105.9 %all-gather.9.cloned.1.call-start = ((), (), s32[]{:S(2)}) async-start(), calls=%async_computation.10 | async-start | bytes 4325376 | tf_op jit(solution)/shard_map/all_gather | solution.py:90
  218.6 35.4 %copy-start = (bf16[128,4096]{0,1:T(8,128)(2,1)S(1)}, bf16[128,4096]{0,1:T(8,128)(2,1)}, u32[]{:S(2)}) copy-start(bf16[128,4096]{0,1:T(8,128)(2,1)} %all-gather.7.cloned.1.call-done) | copy-start | bytes 3145732
  229.3 19.4 %all-to-all-start.5 = ((f32[32,16,128]{2,1,0:T(8,128)}), f32[32,16,128]{2,1,0:T(8,128)S(1)}, u32[]{:S(2)}, u32[]{:S(2)}) async-start(f32[32,16,128]{2,1,0:T(8,128)} %copy.95), calls=%async_computation.5 | async-start | bytes 524288 | tf_op jit(solution)/shard_map/all_to_all | solution.py:55
  248.8 19.5 %all-to-all-start.2 = ((f32[32,16,128]{2,1,0:T(8,128)}), f32[32,16,128]{2,1,0:T(8,128)S(1)}, u32[]{:S(2)}, u32[]{:S(2)}) async-start(f32[32,16,128]{2,1,0:T(8,128)} %copy.85), calls=%async_computation.2 | async-start | bytes 524288 | tf_op jit(solution)/shard_map/all_to_all | solution.py:55
  268.2 36.9 %all-to-all-start.7 = ((bf16[32,128,128]{2,1,0:T(8,128)(2,1)}), bf16[32,128,128]{2,1,0:T(8,128)(2,1)S(1)}, u32[]{:S(2)}, u32[]{:S(2)}) async-start(bf16[32,128,128]{2,1,0:T(8,128)(2,1)} %bitcast.21), calls=%async_computation.7 | async-start | bytes 2097152 | tf_op jit(solution)/shard_map/all_to_all | solution.py:55
Sparse Core Ops, SparseCore 0:
  10.4 43.8 all-gather.6
  56.8 91.7 all-gather.4
  228.3 94.1 all-gather.8

commit v2 on v1

v2 whole, which is shorter than its diff:
```python
import math

import jax
import jax.numpy as jnp
import numpy as np
from jax import lax
from jax.experimental import pallas as pl
from jax.experimental.pallas import tpu as pltpu
from jax.sharding import PartitionSpec as P

PREC = lax.Precision.HIGH
MESH = pl.DeviceIdType.MESH
F32 = jnp.float32
BF16 = jnp.bfloat16
NZ, NY, PARTS, WIDE = 8, 4, 32, 8


def transform_tables(parts, rows):
    total = 2 * parts * rows
    k1 = np.arange(parts + 1)[:, None]
    n1 = np.arange(parts)[None, :]
    turn = 2 * math.pi * ((k1 * n1) % (2 * parts)) / (2 * parts)
    outer = np.concatenate([np.cos(turn), -np.sin(turn)], 0)
    weight = np.full((parts + 1, 1), 2.0)
    weight[0] = weight[-1] = 1.0
    outer_back = np.concatenate([weight * np.cos(turn), -weight * np.sin(turn)], 0).T / total
    n2 = np.arange(rows)
    twist = 2 * math.pi * (k1 * n2[None, :]) / total
    inner = 2 * math.pi * ((n2[:, None] * n2[None, :]) % rows) / rows
    cos, sin = np.cos(inner), np.sin(inner)
    ahead = np.block([[cos, -sin], [sin, cos]])
    back = np.block([[cos, sin], [-sin, cos]])
    return tuple(
        np.asarray(a, np.float32)
        for a in (outer, outer_back, np.cos(twist), np.sin(twist), ahead, back)
    )


def forward(x, tables):
    outer, _, tc, ts, ahead, _ = tables
    parts, c, rows = x.shape
    y = jnp.einsum("kp,pcn->kcn", outer, x, precision=PREC)
    re, im = y[: parts + 1], y[parts + 1 :]
    tc, ts = tc[:, None, :], ts[:, None, :]
    z = jnp.concatenate([re * tc + im * ts, im * tc - re * ts], -1)
    z = jnp.einsum("kcn,nm->kcm", z, ahead, precision=PREC)
    return z[..., :rows], z[..., rows:]


def inverse(re, im, tables):
    _, outer_back, tc, ts, _, back = tables
    rows = re.shape[-1]
    z = jnp.einsum("kcn,nm->kcm", jnp.concatenate([re, im], -1), back, precision=PREC)
    re, im = z[..., :rows], z[..., rows:]
    tc, ts = tc[:, None, :], ts[:, None, :]
    z = jnp.concatenate([re * tc - im * ts, im * tc + re * ts], 0)
    return jnp.einsum("pk,kcn->pcn", outer_back, z, precision=PREC)


class Wire:
    def __init__(self, send, recv):
        self.send, self.recv, self.made = send, recv, []

    def go(self, src, dst, to, there=None):
        i = len(self.made)
        copy = pltpu.make_async_remote_copy(
            src_ref=src,
            dst_ref=dst,
            send_sem=self.send.at[i],
            recv_sem=self.recv.at[i if there is None else there],
            device_id=to,
            device_id_type=MESH,
        )
        copy.start()
        self.made.append(copy)
        return copy

    def drain(self):
        for copy in self.made:
            copy.wait_send()


def place(x, z, k):
    return x * 16 + lax.rem(z + NZ, NZ) * 2 + k


def gather_seq(wire, buf, x, z, k):
    rows = buf.shape[1]
    half, quarter = rows // 2, rows // 4
    low, high, full = (0, half), (half, half), (0, rows)

    def send(src_x, src_z, part, dst):
        ref = buf.at[place(src_x, src_z, k), pl.ds(*part)]
        return wire.go(ref, ref, {"seq": place(*dst)})

    sib, par, right, left = (x, z, 1 - k), (1 - x, z, k), (x, z + 1, k), (x, z - 1, k)
    other = 1 - x
    siblings, across = [], []
    r = send(x, z, full, right)
    l = send(x, z, full, left)
    first = send(x, z, full, par)
    siblings.append(send(x, z, full, sib))
    yield
    first.wait_recv()
    pr = send(other, z, low, right)
    pl_ = send(other, z, low, left)
    siblings.append(send(other, z, full, sib))
    yield
    for j in (1, 2, 3):
        r.wait_recv()
        r = send(x, z - j, full if j < 3 else low, right)
        across.append((z - j, send(x, z - j, high, par)))
        siblings.append(send(x, z - j, full, sib))
        l.wait_recv()
        l = send(x, z + j, full if j < 3 else high, left)
        across.append((z + j, send(x, z + j, high, par)))
        siblings.append(send(x, z + j, full, sib))
        pr.wait_recv()
        pr = send(other, z - j, low if j < 3 else (0, quarter), right)
        siblings.append(send(other, z - j, low, sib))
        pl_.wait_recv()
        pl_ = send(other, z + j, low if j < 3 else (quarter, quarter), left)
        siblings.append(send(other, z + j, low, sib))
        yield
    l.wait_recv()
    across.append((z + 4, send(x, z + 4, high, par)))
    siblings.append(send(x, z + 4, high, sib))
    r.wait_recv()
    siblings.append(send(x, z + 4, low, sib))
    pr.wait_recv()
    pl_.wait_recv()
    siblings.append(send(other, z + 4, low, sib))
    yield
    for far, copy in across:
        copy.wait_recv()
        siblings.append(send(other, far, high, sib))
    yield
    for copy in siblings:
        copy.wait_recv()
    yield


def gather_ch(wire, buf, y, x):
    half = buf.shape[1] // 2

    def send(src_y, src_x, part, dst_y, dst_x):
        ref = buf.at[lax.rem(src_y + NY, NY) * 2 + src_x, pl.ds(*part)]
        return wire.go(ref, ref, {"ch": lax.rem(dst_y + NY, NY) * 2 + dst_x})

    full, low, high = (0, 2 * half), (0, half), (half, half)
    first = send(y, x, full, y, 1 - x)
    near = [send(y, x, full, y + 1, x), send(y, x, full, y - 1, x)]
    yield
    first.wait_recv()
    near += [send(y, 1 - x, full, y + 1, x), send(y, 1 - x, full, y - 1, x)]
    yield
    far = []
    for i, copy in enumerate(near):
        copy.wait_recv()
        whose = x if i < 2 else 1 - x
        if i % 2 == 0:
            far.append(send(y - 1, whose, low, y + 1, x))
        else:
            far.append(send(y + 1, whose, high, y - 1, x))
    yield
    for copy in far:
        copy.wait_recv()
    yield


def advance(steps, count=1):
    for _ in range(count):
        next(steps, None)


def finish(steps):
    for _ in steps:
        pass


class Swap:
    def __init__(self, src, dst, send, recv, me):
        self.src, self.dst, self.send, self.recv, self.me = src, dst, send, recv, me

    def copy(self, d):
        target = lax.rem(self.me + d, PARTS)
        return pltpu.make_async_remote_copy(
            src_ref=self.src.at[target],
            dst_ref=self.dst.at[self.me],
            send_sem=self.send.at[d],
            recv_sem=self.recv.at[d],
            device_id={"seq": target},
            device_id_type=MESH,
        )

    def start(self):
        @pl.loop(1, PARTS)
        def _(d):
            self.copy(d).start()

        self.dst[self.me] = self.src[self.me]

    def wait(self):
        @pl.loop(1, PARTS)
        def _(d):
            self.copy(d).wait()


def envelope_of(rates, me, rows):
    total = rows * PARTS
    spot = me * rows + lax.broadcasted_iota(jnp.int32, (rows, 1), 0)
    spot = spot.astype(F32) / total
    scaling = jnp.sqrt(2.0 * rates / (total * (1.0 - jnp.exp(-2.0 * rates))))
    return jnp.exp(-spot * rates) * scaling


def greet(me, extra):
    barrier = pltpu.get_barrier_semaphore()

    @pl.loop(1, PARTS)
    def _(d):
        pl.semaphore_signal(
            barrier, inc=1, device_id={"seq": lax.rem(me + d, PARTS)}, device_id_type=MESH
        )

    for to in extra:
        pl.semaphore_signal(barrier, inc=1, device_id=to, device_id_type=MESH)
    pl.semaphore_wait(barrier, PARTS - 1 + len(extra))


def opening(
    q_ref, k_ref, v_ref, f_ref, rates_ref, w_ref, c_ref,
    pf_out, gm_out, q_out, gg_out, tall,
    wbuf, cbuf, pf_src, gm_src, q_src,
    wire_send, wire_recv, swap_send, swap_recv,
):
    me, ch = lax.axis_index("seq"), lax.axis_index("ch")
    x, z, k = me // 16, lax.rem(me // 2, NZ), lax.rem(me, 2)
    y, xl = ch // 2, lax.rem(ch, 2)
    rows, chans = q_ref.shape
    fine = chans // PARTS
    wire = Wire(wire_send, wire_recv)

    wbuf[me] = w_ref[...]
    cbuf[ch] = c_ref[...]
    keeper = lax.rem(me // 4 + 1 + lax.rem(me, 4), WIDE)
    targets = [{"seq": ch * 4 + i, "ch": keeper} for i in range(4)]
    sources = [
        {"seq": 4 * lax.rem(ch - 1 - j + WIDE, WIDE) + j, "ch": me // 4} for j in range(4)
    ]
    around = [
        {"ch": y * 2 + 1 - xl},
        {"ch": lax.rem(y + 1, NY) * 2 + xl},
        {"ch": lax.rem(y + NY - 1, NY) * 2 + xl},
    ]
    greet(me, targets + sources + around)

    weights = gather_seq(wire, wbuf, x, z, k)
    advance(weights)
    wide = gather_ch(wire, cbuf, y, xl)
    advance(wide)
    base = len(wire.made)
    for i, to in enumerate(targets):
        src = cbuf.at[ch, :, pl.ds(i * 128, 128)]
        wire.go(src, tall.at[keeper, lax.rem(me, 4)], to, base + lax.rem(me, 4))

    env = envelope_of(rates_ref[...], me, rows)
    product = k_ref[...].astype(F32) * v_ref[...].astype(F32)
    pf_src[:, 0] = product.T.reshape(PARTS, fine, rows)
    pf_src[:, 1] = (f_ref[...] * env).T.reshape(PARTS, fine, rows)
    q_src[...] = q_ref[...].astype(F32).T.reshape(PARTS, fine, rows).astype(BF16)

    advance(weights)
    advance(wide)
    advance(weights)
    advance(wide)
    for j in range(4):
        pltpu.make_async_copy(tall.at[0, 0], tall.at[0, 0], wire_recv.at[base + j]).wait()
    high = gather_ch(wire, tall, y, xl)
    advance(high)
    advance(weights)
    advance(wide)
    advance(high)
    advance(weights)
    pf = Swap(pf_src, pf_out, swap_send.at[0], swap_recv.at[0], me)
    qs = Swap(q_src, q_out, swap_send.at[1], swap_recv.at[1], me)
    gm = Swap(gm_src, gm_out, swap_send.at[2], swap_recv.at[2], me)
    pf.start()
    qs.start()
    advance(high)
    finish(weights)
    finish(wide)
    total = jnp.zeros((rows, chans), F32)
    for h in range(WIDE):
        part = jnp.concatenate([wbuf[4 * h + i] for i in range(4)], axis=1)
        total += lax.dot_general(
            cbuf[h], part, (((1,), (1,)), ((), ())), preferred_element_type=F32
        )
    gg_out[...] = total
    gm_src[...] = (q_ref[...].astype(F32) * total).T.reshape(PARTS, fine, rows)
    gm.start()
    finish(high)
    pf.wait()
    qs.wait()
    gm.wait()
    wire.drain()


def closing(
    gated_ref, mixed_ref, prod_ref, taps_ref, gg_ref, k_ref, v_ref, rates_ref, tall_ref,
    gq_out, gk_out, gv_out, gf_out, gw_out,
    gbuf, mixed_in, prod_in, taps_in,
    wire_send, wire_recv, swap_send, swap_recv,
):
    me = lax.axis_index("seq")
    x, z, k = me // 16, lax.rem(me // 2, NZ), lax.rem(me, 2)
    rows, chans = k_ref.shape
    fine = chans // PARTS
    wire = Wire(wire_send, wire_recv)
    gbuf[me] = gated_ref[...]
    greet(me, [])
    steps = gather_seq(wire, gbuf, x, z, k)
    advance(steps, 5)
    swaps = [
        Swap(src, dst, swap_send.at[i], swap_recv.at[i], me)
        for i, (src, dst) in enumerate(
            ((mixed_ref, mixed_in), (prod_ref, prod_in), (taps_ref, taps_in))
        )
    ]
    for swap in swaps:
        swap.start()
    env = envelope_of(rates_ref[...], me, rows)
    finish(steps)
    total = jnp.zeros(gw_out.shape, F32)
    for a in range(WIDE):
        left, right = [], []
        for j in range(4):
            block = 4 * a + j
            left.append(gbuf[:, pl.ds(block * fine, fine), :].reshape(chans, rows))
            right.append(tall_ref[(a + 1 + j) % WIDE, j])
        total += jnp.dot(
            jnp.concatenate(left, axis=1),
            jnp.concatenate(right, axis=0),
            preferred_element_type=F32,
        )
    gw_out[...] = total
    swaps[0].wait()
    gq_out[...] = (mixed_in[...].reshape(chans, rows).T * gg_ref[...]).astype(BF16)
    swaps[1].wait()
    back = prod_in[...].reshape(chans, rows).T
    gk_out[...] = (back * v_ref[...].astype(F32)).astype(BF16)
    gv_out[...] = (back * k_ref[...].astype(F32)).astype(BF16)
    swaps[2].wait()
    gf_out[...] = taps_in[...].reshape(chans, rows).T * env
    wire.drain()


def on_device(query, key, value, filter_raw, rates, out_weight, cotangent):
    rows, chans = query.shape
    fine = chans // PARTS
    tables = transform_tables(PARTS, rows)
    rates = rates.reshape(1, chans)
    vmem = pl.BlockSpec(memory_space=pltpu.VMEM)
    shape = jax.ShapeDtypeStruct
    piece = (PARTS, fine, rows)
    sems = [
        pltpu.SemaphoreType.DMA((80,)),
        pltpu.SemaphoreType.DMA((80,)),
        pltpu.SemaphoreType.DMA((3, PARTS)),
        pltpu.SemaphoreType.DMA((3, PARTS)),
    ]
    pf, gm, query_c, grad_gated, tall = pl.pallas_call(
        opening,
        out_shape=(
            shape((PARTS, 2, fine, rows), F32),
            shape(piece, F32),
            shape(piece, BF16),
            shape((rows, chans), F32),
            shape((WIDE, 4, rows, out_weight.shape[1]), BF16),
        ),
        in_specs=[vmem] * 7,
        out_specs=(vmem,) * 5,
        scratch_shapes=[
            pltpu.VMEM((PARTS, chans, out_weight.shape[1]), BF16),
            pltpu.VMEM((WIDE, rows, chans), BF16),
            pltpu.VMEM((PARTS, 2, fine, rows), F32),
            pltpu.VMEM(piece, F32),
            pltpu.VMEM(piece, BF16),
        ]
        + sems,
        compiler_params=pltpu.CompilerParams(
            collective_id=0, has_side_effects=True, vmem_limit_bytes=40 * 2**20
        ),
        name="opening",
    )(query, key, value, filter_raw, rates, out_weight, cotangent)

    pr, pi = forward(pf[:, 0], tables)
    fr, fi = forward(pf[:, 1], tables)
    gr, gi = forward(gm, tables)
    mixed = inverse(pr * fr - pi * fi, pr * fi + pi * fr, tables)
    gated = (query_c.astype(F32) * mixed).astype(BF16).reshape(chans, rows)
    grad_product = inverse(gr * fr + gi * fi, gi * fr - gr * fi, tables)
    grad_taps = inverse(gr * pr + gi * pi, gi * pr - gr * pi, tables)

    return pl.pallas_call(
        closing,
        out_shape=(
            shape((rows, chans), BF16),
            shape((rows, chans), BF16),
            shape((rows, chans), BF16),
            shape((rows, chans), F32),
            shape(out_weight.shape, F32),
        ),
        in_specs=[vmem] * 9,
        out_specs=(vmem,) * 5,
        scratch_shapes=[pltpu.VMEM((PARTS, chans, rows), BF16)] + [pltpu.VMEM(piece, F32)] * 3 + sems,
        compiler_params=pltpu.CompilerParams(
            collective_id=1, has_side_effects=True, vmem_limit_bytes=40 * 2**20
        ),
        name="closing",
    )(gated, mixed, grad_product, grad_taps, grad_gated, key, value, rates, tall)


def solution(mesh):
    return jax.shard_map(
        on_device,
        mesh=mesh,
        in_specs=(
            P("seq", "ch"),
            P("seq", "ch"),
            P("seq", "ch"),
            P("seq", "ch"),
            P("ch"),
            P("ch", "seq"),
            P("seq", "ch"),
        ),
        out_specs=(P("seq", "ch"), P("seq", "ch"), P("seq", "ch"), P("seq", "ch"), P("ch", "seq")),
        check_vma=False,
    )
```

time: 335 us -> 131 us (0.39)
  waiting for transfers between devices: 229 us -> 0 us
  Pallas kernels: 0 us -> 109 us
  starting transfers between devices: 43.1 us -> 0 us
  blocking collectives: 17.7 us -> 0 us
  between operations: 14.1 us -> 0.9 us
  matrix products: 16.1 us -> 5.7 us
    all_gather x3 -> x0, waiting for transfers between devices: 139 us -> none  [the longest x1 94.3 us: on_device(): wide_weight = lax.all_gather(out_weight, 'seq', axis=1, tiled=True)]
    pallas_call x0 -> x2, Pallas kernels: none -> 109 us  [the longest x1 62.6 us: on_device(): pl.pallas_call(opening, out_shape=(shape((PARTS, 2, fine, rows), F32), sh...]
    all_to_all x7 -> x0, waiting for transfers between devices: 88.6 us -> none  [exchange(): return lax.all_to_all(x, 'seq', 0, 0, tiled=True)]
    all_to_all x7 -> x0, starting transfers between devices: 43 us -> none  [exchange(): return lax.all_to_all(x, 'seq', 0, 0, tiled=True)]
    all_to_all x1 -> x0, blocking collectives: 17.7 us -> none  [exchange(): return lax.all_to_all(x, 'seq', 0, 0, tiled=True)]
    dot_general x2 -> x0, matrix products: 9.72 us -> none  [the longest x1 5.25 us: on_device(): jnp.einsum('sptr,pro->sto', all_gated.transpose(0, 1, 2, 3), tall_cot, pr...]
    unnamed x27 -> x37, local copies, waits for them, and re-layouts: 7.86 us -> 13.5 us
  transfers between devices with their start and end apart: 10 -> 0, of which waited for: 9 -> 0; matrix products, arithmetic and copies ran while one was open for 6% -> 0% of each run, Pallas kernels for 0% -> 0%
where the time goes in v2:
time: 131 us
  Pallas kernels  109 us (83%)
  local copies, waits for them, and re-layouts  13.9 us (11%)
  matrix products  5.7 us (4%)
    pallas_call x1, Pallas kernels, on_device(): pl.pallas_call(opening, out_shape=(shape((PARTS, 2, fine, rows), F32), sh...  62.6 us
    pallas_call x1, Pallas kernels, on_device(): pl.pallas_call(closing, out_shape=(shape((rows, chans), BF16), shape((row...  46.7 us
    unnamed x37, local copies, waits for them, and re-layouts  13.5 us

profile of v2, /device:TPU:1, one launch (start us, length us, event | category | flops | bytes accessed | tf_op | source)
XLA Modules:
  0.0 130.9 jit_solution(4371948563526430381)
XLA Ops:
  0.6 0.9 copy-done
  1.5 0.9 copy-done.2
  2.4 0.9 copy-done.4
  3.4 0.9 copy-done.5
  4.3 0.9 copy-done.6
  5.2 0.9 copy-done.7
  6.1 0.7 copy-done.8
  6.8 62.6 %opening.1 = (f32[32,2,16,128]{3,2,1,0:T(8,128)S(1)}, f32[32,16,128]{2,1,0:T(8,128)S(1)}, bf16[32,16,128]{2,1,0:T(8,128)(2,1)S(1)}, f32[128,512]{1,0:T(8,128)S(1)}, bf16[8,4,128,128]{3,2,1,0:T(8,128)(2,1)S(1)}) custom-call(bf16[128,512]{1,0:T(8,128)(2,1)S(1)} %copy-done.5, bf16[128,512]{1,0:T(8,128)(2,1)S(1)} %copy-done, bf16[128,512]{1,0:T(8,128)(2,1)S(1)} %copy-done.2, ...), custom_call_target="tpu_custom_call" | custom-call | tf_op jit(solution)/shard_map/opening/pallas_call | solution.py:372
  69.4 0.0 copy-start.13
  69.5 0.7 copy-done.13
  70.1 0.4 fusion.28
  70.6 0.4 fusion.26
  71.0 0.0 copy-start.14
  71.0 0.0 copy-start.15
  71.0 0.4 fusion.24
  71.5 0.3 copy-done.14
  71.8 0.0 copy-done.15
  71.8 0.3 multiply_add_fusion.2
  72.0 0.0 copy-start.11
  72.1 0.9 copy-done.11
  73.0 0.5 fusion.18
  73.5 0.1 pad_maximum_fusion
  73.6 0.5 fusion.22
  74.1 0.5 fusion.20
  74.6 0.1 multiply_add_fusion.6
  74.7 0.1 multiply_add_fusion.7
  74.8 0.1 pad_maximum_fusion.4
  74.9 0.1 pad_maximum_fusion.5
  74.9 0.9 copy-done.10
  75.8 0.7 fusion
  76.5 0.7 fusion.2
  77.2 0.7 fusion.4
  77.9 0.2 multiply_subtract_fusion
  78.1 0.5 copy-done.12
  78.6 0.3 fusion.14
  78.9 0.2 copy.51.taps_ref
  79.1 0.3 fusion.6
  79.4 0.3 fusion.10
  79.7 0.2 copy.50.prod_ref
  79.9 0.2 fusion.33
  80.1 0.7 copy-done.1
  80.8 0.1 copy-done.3
  80.8 46.7 %closing.1 = (bf16[128,512]{1,0:T(8,128)(2,1)S(1)}, bf16[128,512]{1,0:T(8,128)(2,1)S(1)}, bf16[128,512]{1,0:T(8,128)(2,1)S(1)}, f32[128,512]{1,0:T(8,128)S(1)}, f32[512,128]{1,0:T(8,128)S(1)}) custom-call(bf16[512,128]{1,0:T(8,128)(2,1)S(1)} %bitcast.22, f32[32,16,128]{2,1,0:T(8,128)S(1)} %get-tuple-element.37.mixed_ref, f32[32,16,128]{2,1,0:T(8,128)S(1)} %copy.50.prod_ref, ...), custom_call_target="tpu_custom_call" | custom-call | tf_op jit(solution)/shard_map/closing/pallas_call | solution.py:405
  127.5 0.7 copy.83
  128.2 0.7 copy.84
  128.9 0.7 copy.85
  129.5 0.7 copy.86
  130.2 0.7 copy.87
  (16 shorter events, 0.2 us)
Async XLA Ops:
  0.6 0.9 copy-start
  1.5 0.9 copy-start.2
  2.4 0.9 copy-start.4
  3.4 0.9 copy-start.5
  4.3 0.9 copy-start.6
  5.2 0.9 copy-start.7
  6.1 0.7 copy-start.8
  69.4 0.7 copy-start.13
  71.0 0.7 copy-start.14
  71.0 0.7 copy-start.15
  72.0 1.0 copy-start.11
  74.9 1.0 copy-start.10
  77.9 0.7 copy-start.12
  79.8 0.9 copy-start.1
  79.9 1.0 copy-start.3
  80.0 0.8 copy-start.9

commit v3 on v2

v3 whole, which is shorter than its diff:
```python
import math

import jax
import jax.numpy as jnp
import numpy as np
from jax import lax
from jax.experimental import pallas as pl
from jax.experimental.pallas import tpu as pltpu
from jax.sharding import PartitionSpec as P

MESH = pl.DeviceIdType.MESH
F32 = jnp.float32
BF16 = jnp.bfloat16
NZ, NY, PARTS, WIDE = 8, 4, 32, 8


def transform_tables(rows):
    total = 2 * PARTS * rows
    k1 = np.arange(PARTS + 1)[:, None]
    n1 = np.arange(PARTS)[None, :]
    turn = 2 * math.pi * ((k1 * n1) % (2 * PARTS)) / (2 * PARTS)
    eye = np.eye(8)
    outer = np.kron(np.concatenate([np.cos(turn), -np.sin(turn)[1:-1]], 0), eye)
    weight = np.full((PARTS + 1, 1), 2.0)
    weight[0] = weight[-1] = 1.0
    outer_back = np.concatenate([weight * np.cos(turn), (-weight * np.sin(turn))[1:-1]], 0)
    outer_back = np.kron(outer_back.T / total, eye)
    n2 = np.arange(rows)
    twist = np.repeat(2 * math.pi * (k1 * n2[None, :]) / total, 8, axis=0)
    inner = 2 * math.pi * ((n2[:, None] * n2[None, :]) % rows) / rows
    cos, sin = np.cos(inner), np.sin(inner)
    ahead = np.block([[cos, -sin], [sin, cos]])
    back = np.block([[cos, sin], [-sin, cos]])

    def pair(m):
        high = np.asarray(m, np.float32).astype(BF16)
        low = (m - high.astype(np.float64)).astype(BF16)
        return np.stack([high, low])

    turns = np.stack([np.cos(twist), np.sin(twist)]).astype(np.float32)
    return pair(outer), pair(outer_back), np.concatenate([pair(ahead), pair(back)]), turns


def halves(x):
    high = x.astype(BF16)
    return high, (x - high.astype(F32)).astype(BF16)


def dot(a, b):
    return jnp.dot(a, b, preferred_element_type=F32)


def dot_const_left(const, x):
    high, low = halves(x)
    return dot(const[0], high) + dot(const[0], low) + dot(const[1], high)


def dot_const_right(x, const, at):
    high, low = halves(x)
    return dot(high, const[at]) + dot(low, const[at]) + dot(high, const[at + 1])


def forward(signals, outer, inner, turns):
    groups = [x[:, 8 * i : 8 * i + 8, :].reshape(256, 128) for x in signals for i in range(2)]
    y = dot_const_left(outer, jnp.concatenate(groups, axis=1))
    cos, sin = turns[0], turns[1]
    rest = jnp.zeros((8, 128), F32)
    rows = []
    for i in range(len(groups)):
        part = y[:, 128 * i : 128 * i + 128]
        re, im = part[:264], jnp.concatenate([rest, part[264:], rest], axis=0)
        rows.append(jnp.concatenate([re * cos + im * sin, im * cos - re * sin], axis=1))
    z = dot_const_right(jnp.concatenate(rows, axis=0), inner, 0)
    return [(z[528 * i : 528 * i + 528, :128], z[528 * i : 528 * i + 528, 128:]) for i in range(len(signals))]


def inverse(spectra, outer_back, inner, turns):
    z = jnp.concatenate([jnp.concatenate(pair, axis=1) for pair in spectra], axis=0)
    z = dot_const_right(z, inner, 2)
    cos, sin = turns[0], turns[1]
    columns = []
    for i in range(2 * len(spectra)):
        re, im = z[264 * i : 264 * i + 264, :128], z[264 * i : 264 * i + 264, 128:]
        columns.append(jnp.concatenate([re * cos - im * sin, (im * cos + re * sin)[8:256]], axis=0))
    y = dot_const_left(outer_back, jnp.concatenate(columns, axis=1))
    groups = [y[:, 128 * i : 128 * i + 128].reshape(PARTS, 8, 128) for i in range(len(columns))]
    return [jnp.concatenate(groups[2 * i : 2 * i + 2], axis=1) for i in range(len(spectra))]


def pack(x, scale):
    x = x * scale
    square = x * x
    return (square * (x * jnp.abs(x))).astype(BF16)


def unpack(code, scale):
    code = code.astype(F32)
    size = jnp.sqrt(jnp.sqrt(jnp.abs(code))) * (1.0 / scale)
    return jnp.where(code < 0.0, -size, size)


class Wire:
    def __init__(self, send, recv):
        self.send, self.recv, self.made = send, recv, []

    def go(self, src, dst, to, there=None):
        i = len(self.made)
        copy = pltpu.make_async_remote_copy(
            src_ref=src,
            dst_ref=dst,
            send_sem=self.send.at[i],
            recv_sem=self.recv.at[i if there is None else there],
            device_id=to,
            device_id_type=MESH,
        )
        copy.start()
        self.made.append(copy)
        return copy

    def drain(self):
        for copy in self.made:
            copy.wait_send()


def place(x, z, k):
    return x * 16 + lax.rem(z + NZ, NZ) * 2 + k


def gather_seq(wire, buf, x, z, k):
    rows = buf.shape[1]
    half, quarter = rows // 2, rows // 4
    low, high, full = (0, half), (half, half), (0, rows)

    def send(src_x, src_z, part, dst):
        ref = buf.at[place(src_x, src_z, k), pl.ds(*part)]
        return wire.go(ref, ref, {"seq": place(*dst)})

    sib, par, right, left = (x, z, 1 - k), (1 - x, z, k), (x, z + 1, k), (x, z - 1, k)
    other = 1 - x
    siblings, across = [], []
    r = send(x, z, full, right)
    l = send(x, z, full, left)
    first = send(x, z, full, par)
    siblings.append(send(x, z, full, sib))
    yield
    first.wait_recv()
    pr = send(other, z, low, right)
    pl_ = send(other, z, low, left)
    siblings.append(send(other, z, full, sib))
    yield
    for j in (1, 2, 3):
        r.wait_recv()
        r = send(x, z - j, full if j < 3 else low, right)
        across.append((z - j, send(x, z - j, high, par)))
        siblings.append(send(x, z - j, full, sib))
        l.wait_recv()
        l = send(x, z + j, full if j < 3 else high, left)
        across.append((z + j, send(x, z + j, high, par)))
        siblings.append(send(x, z + j, full, sib))
        pr.wait_recv()
        pr = send(other, z - j, low if j < 3 else (0, quarter), right)
        siblings.append(send(other, z - j, low, sib))
        pl_.wait_recv()
        pl_ = send(other, z + j, low if j < 3 else (quarter, quarter), left)
        siblings.append(send(other, z + j, low, sib))
        yield
    l.wait_recv()
    across.append((z + 4, send(x, z + 4, high, par)))
    siblings.append(send(x, z + 4, high, sib))
    r.wait_recv()
    siblings.append(send(x, z + 4, low, sib))
    pr.wait_recv()
    pl_.wait_recv()
    siblings.append(send(other, z + 4, low, sib))
    yield
    for far, copy in across:
        copy.wait_recv()
        siblings.append(send(other, far, high, sib))
    yield
    for copy in siblings:
        copy.wait_recv()
    yield


def ring_z(wire, buf, x, z, k, across):
    def ref(far, *part):
        return buf.at[(lax.rem(z + far + NZ, NZ) * 2 + k, *part)]

    def send(far, part, step):
        r = ref(far, part)
        return wire.go(r, r, {"seq": place(x, z + step, k)})

    def share(far, *part):
        r = ref(far, *part)
        return wire.go(r, r, {"seq": place(x, z, 1 - k)})

    other = 1 - x
    right, left = send(0, x, 1), send(0, x, -1)
    siblings = [share(0, x)]
    yield
    across.wait_recv()
    right2, left2 = send(0, other, 1), send(0, other, -1)
    siblings.append(share(0, other))
    yield
    for j in (1, 2, 3):
        right.wait_recv()
        right = send(-j, x, 1)
        left.wait_recv()
        left = send(j, x, -1) if j < 3 else None
        right2.wait_recv()
        right2 = send(-j, other, 1) if j < 3 else None
        left2.wait_recv()
        left2 = send(j, other, -1)
        siblings += [share(-j), share(j)]
        yield
    right.wait_recv()
    left2.wait_recv()
    siblings.append(share(4))
    yield
    for copy in siblings:
        copy.wait_recv()
    yield


def gather_ch(wire, buf, y, x):
    half = buf.shape[1] // 2

    def send(src_y, src_x, part, dst_y, dst_x):
        ref = buf.at[lax.rem(src_y + NY, NY) * 2 + src_x, pl.ds(*part)]
        return wire.go(ref, ref, {"ch": lax.rem(dst_y + NY, NY) * 2 + dst_x})

    full, low, high = (0, 2 * half), (0, half), (half, half)
    first = send(y, x, full, y, 1 - x)
    near = [send(y, x, full, y + 1, x), send(y, x, full, y - 1, x)]
    yield
    first.wait_recv()
    near += [send(y, 1 - x, full, y + 1, x), send(y, 1 - x, full, y - 1, x)]
    yield
    far = []
    for i, copy in enumerate(near):
        copy.wait_recv()
        whose = x if i < 2 else 1 - x
        if i % 2 == 0:
            far.append(send(y - 1, whose, low, y + 1, x))
        else:
            far.append(send(y + 1, whose, high, y - 1, x))
    yield
    for copy in far:
        copy.wait_recv()
    yield


def advance(steps, count=1):
    for _ in range(count):
        next(steps, None)


def finish(steps):
    for _ in steps:
        pass


class Swap:
    def __init__(self, src, dst, send, recv, me):
        self.src, self.dst, self.send, self.recv, self.me = src, dst, send, recv, me

    def copy(self, d):
        target = lax.rem(self.me + d, PARTS)
        return pltpu.make_async_remote_copy(
            src_ref=self.src.at[target],
            dst_ref=self.dst.at[self.me],
            send_sem=self.send.at[d],
            recv_sem=self.recv.at[d],
            device_id={"seq": target},
            device_id_type=MESH,
        )

    def start(self, low=1, high=PARTS):
        @pl.loop(low, high)
        def _(d):
            self.copy(d).start()

        if low == 1:
            self.dst[self.me] = self.src[self.me]

    def wait(self):
        @pl.loop(1, PARTS)
        def _(d):
            self.copy(d).wait()


def envelope_of(rates, me, rows):
    total = rows * PARTS
    spot = me * rows + lax.broadcasted_iota(jnp.int32, (rows, 1), 0)
    spot = spot.astype(F32) / total
    scaling = jnp.sqrt(2.0 * rates / (total * (1.0 - jnp.exp(-2.0 * rates))))
    return jnp.exp(-spot * rates) * scaling


def whole(
    q_hbm, k_hbm, v_hbm, f_hbm, r_hbm, w_hbm, c_hbm, outer_hbm, back_hbm, inner_hbm, turns_hbm,
    gq_out, gk_out, gv_out, gf_out, gw_out,
    q_ref, k_ref, v_ref, f_ref, r_ref, outer, back, inner, turns,
    wbuf, cbuf, tall, gbuf, gg_ref, rate_ref,
    in_src, in_dst, gm_src, gm_dst, home_src, home_dst, gated_ref, half_src, half_dst,
    load_sem, wire_send, wire_recv, swap_send, swap_recv,
):
    me, ch = lax.axis_index("seq"), lax.axis_index("ch")
    x, z, k = me // 16, lax.rem(me // 2, NZ), lax.rem(me, 2)
    zk = lax.rem(me, 16)
    y, xl = ch // 2, lax.rem(ch, 2)
    rows, chans = q_ref.shape
    fine = chans // PARTS
    wire = Wire(wire_send, wire_recv)

    loads = [
        pltpu.make_async_copy(src, dst, load_sem.at[i])
        for i, (src, dst) in enumerate(
            (
                (w_hbm, wbuf.at[me]),
                (c_hbm, cbuf.at[ch]),
                (k_hbm, k_ref),
                (v_hbm, v_ref),
                (f_hbm, f_ref),
                (q_hbm, q_ref),
                (r_hbm, r_ref),
                (outer_hbm, outer),
                (back_hbm, back),
                (inner_hbm, inner),
                (turns_hbm, turns),
            )
        )
    ]
    for load in loads:
        load.start()

    spot = (ch // 4) * 16 + zk
    keeper = lax.rem(spot // 4 + 1 + lax.rem(spot, 4), WIDE)
    targets = [{"seq": x * 16 + lax.rem(ch, 4) * 4 + i, "ch": keeper} for i in range(4)]
    sources = []
    for j in range(4):
        theirs = 4 * lax.rem(ch - 1 - j + WIDE, WIDE) + j
        sources.append(
            {"seq": x * 16 + lax.rem(theirs, 16), "ch": (theirs // 16) * 4 + zk // 4}
        )
    around = [
        {"ch": y * 2 + 1 - xl},
        {"ch": lax.rem(y + 1, NY) * 2 + xl},
        {"ch": lax.rem(y + NY - 1, NY) * 2 + xl},
    ]
    greeted = targets + sources + around
    barrier = pltpu.get_barrier_semaphore()

    @pl.loop(1, PARTS)
    def _(d):
        pl.semaphore_signal(
            barrier, inc=1, device_id={"seq": lax.rem(me + d, PARTS)}, device_id_type=MESH
        )

    for to in greeted:
        pl.semaphore_signal(barrier, inc=1, device_id=to, device_id_type=MESH)

    for load in loads:
        load.wait()

    def turned(value):
        return value.T.reshape(PARTS, fine, rows)

    in_src[:, 0:16] = pack(turned(k_ref[...].astype(F32) * v_ref[...].astype(F32)), 2.0**25)
    in_src[:, 16:32] = pack(turned(f_ref[...]), 2.0**28)
    in_src[:, 32:48] = turned(q_ref[...].astype(F32)).astype(BF16)
    rate_ref[...] = jnp.broadcast_to(r_ref[...], (rows, chans)).T
    env = envelope_of(r_ref[...], me, rows)
    own_rates = rate_ref[pl.ds(me * fine, fine), :]
    lanes = lax.broadcasted_iota(jnp.int32, (fine, rows), 1)
    span = float(rows * PARTS)
    own_scaling = jnp.sqrt(2.0 * own_rates / (span * (1.0 - jnp.exp(-2.0 * own_rates))))
    envelope = jnp.stack(
        [
            jnp.exp(-((lanes + block * rows).astype(F32) / span) * own_rates) * own_scaling
            for block in range(PARTS)
        ]
    )
    pl.semaphore_wait(barrier, PARTS - 1 + len(greeted))

    weights = gather_seq(wire, wbuf, x, z, k)
    advance(weights)
    wide = gather_ch(wire, cbuf, y, xl)
    advance(wide)
    base = len(wire.made)
    for i, to in enumerate(targets):
        src = cbuf.at[ch, :, pl.ds(i * 128, 128)]
        wire.go(src, tall.at[keeper, lax.rem(me, 4)], to, base + lax.rem(me, 4))

    def swap(i, src, dst):
        return Swap(src, dst, swap_send.at[i], swap_recv.at[i], me)

    early = swap(0, in_src, in_dst)
    late = swap(1, gm_src, gm_dst)
    homes = [swap(2 + i, home_src.at[i], home_dst.at[i]) for i in range(3)]

    early.start(1, 12)
    advance(weights)
    advance(wide)
    early.start(12, 22)
    advance(weights)
    advance(wide)
    early.start(22, PARTS)
    advance(weights)
    for j in range(4):
        pltpu.make_async_copy(tall.at[0, 0], tall.at[0, 0], wire_recv.at[base + j]).wait()
    high = gather_ch(wire, tall, y, xl)
    advance(high)
    advance(weights)
    advance(wide)
    advance(high)
    advance(weights)
    advance(high)

    early.wait()
    product = unpack(in_dst[:, 0:16], 2.0**25)
    filt = unpack(in_dst[:, 16:32], 2.0**28) * envelope
    (pr, pi), (fr, fi) = forward([product, filt], outer, inner, turns)
    (mixed,) = inverse([(pr * fr - pi * fi, pr * fi + pi * fr)], back, inner, turns)
    gated_ref[...] = (in_dst[:, 32:48].astype(F32) * mixed).astype(BF16)
    across = wire.go(
        gated_ref.at[pl.ds(16 * (1 - x), 16)], gbuf.at[zk, x], {"seq": place(1 - x, z, k)}
    )
    gbuf[zk, x] = gated_ref[pl.ds(16 * x, 16)]
    ring = ring_z(wire, gbuf, x, z, k, across)
    advance(ring)
    home_src[0] = pack(mixed, 2.0**17)
    homes[0].start()

    finish(weights)
    finish(wide)
    total = jnp.zeros((rows, chans), F32)
    for h in range(WIDE):
        part = jnp.concatenate([wbuf[4 * h + i] for i in range(4)], axis=1)
        total += lax.dot_general(
            cbuf[h], part, (((1,), (1,)), ((), ())), preferred_element_type=F32
        )
    gg_ref[...] = total
    gm_src[...] = pack(turned(q_ref[...].astype(F32) * total), 2.0**17)
    late.start()
    advance(ring, 2)
    finish(high)
    late.wait()
    grad = unpack(gm_dst[...], 2.0**17)
    ((gr, gi),) = forward([grad], outer, inner, turns)
    advance(ring)
    back_product, back_taps = inverse(
        [(gr * fr + gi * fi, gi * fr - gr * fi), (gr * pr + gi * pi, gi * pr - gr * pi)],
        back, inner, turns,
    )
    home_src[1] = pack(back_product, 2.0**8)
    homes[1].start()
    home_src[2] = pack(back_taps, 1.0)
    homes[2].start()
    finish(ring)

    total = jnp.zeros((chans, 256), F32)
    for a in range(4):
        left, right = [], []
        for j in range(4):
            block = 4 * a + j
            left.append(
                jnp.concatenate([gbuf[:, i, block].reshape(256, 128) for i in range(2)], axis=0)
            )
            right.append(
                jnp.concatenate([tall[(4 * i + a + 1 + j) % WIDE, j] for i in range(2)], axis=1)
            )
        total += dot(jnp.concatenate(left, axis=1), jnp.concatenate(right, axis=0))
    mine = jnp.where(x == 0, total[:, :128], total[:, 128:])
    theirs = jnp.where(x == 0, total[:, 128:], total[:, :128])
    half_src[...] = pack(theirs, 1.0)
    last = wire.go(half_src, half_dst, {"seq": place(1 - x, z, k)})

    def arrived(i, scale):
        homes[i].wait()
        return unpack(home_dst[i].reshape(chans, rows), scale).T

    gq_out[...] = (arrived(0, 2.0**17) * gg_ref[...]).astype(BF16)
    grad_product = arrived(1, 2.0**8)
    gk_out[...] = (grad_product * v_ref[...].astype(F32)).astype(BF16)
    gv_out[...] = (grad_product * k_ref[...].astype(F32)).astype(BF16)
    gf_out[...] = arrived(2, 1.0) * env
    last.wait_recv()
    gw_out[...] = mine + unpack(half_dst[...], 1.0)
    wire.drain()


def on_device(query, key, value, filter_raw, rates, out_weight, cotangent):
    rows, chans = query.shape
    fine = chans // PARTS
    tables = transform_tables(rows)
    columns = out_weight.shape[1]
    shape = jax.ShapeDtypeStruct
    block = pltpu.VMEM((rows, chans), BF16)
    piece = (PARTS, fine, rows)
    return pl.pallas_call(
        whole,
        out_shape=(
            shape((rows, chans), BF16),
            shape((rows, chans), BF16),
            shape((rows, chans), BF16),
            shape((rows, chans), F32),
            shape(out_weight.shape, F32),
        ),
        in_specs=[pl.BlockSpec(memory_space=pl.ANY)] * 11,
        out_specs=(pl.BlockSpec(memory_space=pltpu.VMEM),) * 5,
        scratch_shapes=[
            block,
            block,
            block,
            pltpu.VMEM((rows, chans), F32),
            pltpu.VMEM((1, chans), F32),
            *(pltpu.VMEM(t.shape, t.dtype) for t in tables),
            pltpu.VMEM((PARTS, chans, columns), BF16),
            pltpu.VMEM((WIDE, rows, chans), BF16),
            pltpu.VMEM((WIDE, 4, rows, columns), BF16),
            pltpu.VMEM((16, 2, 16, fine, rows), BF16),
            pltpu.VMEM((rows, chans), F32),
            pltpu.VMEM((chans, rows), F32),
            pltpu.VMEM((PARTS, 3 * fine, rows), BF16),
            pltpu.VMEM((PARTS, 3 * fine, rows), BF16),
            pltpu.VMEM(piece, BF16),
            pltpu.VMEM(piece, BF16),
            pltpu.VMEM((3, *piece), BF16),
            pltpu.VMEM((3, *piece), BF16),
            pltpu.VMEM(piece, BF16),
            pltpu.VMEM((chans, columns), BF16),
            pltpu.VMEM((chans, columns), BF16),
            pltpu.SemaphoreType.DMA((11,)),
            pltpu.SemaphoreType.DMA((128,)),
            pltpu.SemaphoreType.DMA((128,)),
            pltpu.SemaphoreType.DMA((5, PARTS)),
            pltpu.SemaphoreType.DMA((5, PARTS)),
        ],
        compiler_params=pltpu.CompilerParams(
            collective_id=0, has_side_effects=True, vmem_limit_bytes=48 * 2**20
        ),
        name="whole",
    )(
        query, key, value, filter_raw, rates.reshape(1, chans), out_weight, cotangent,
        *(jnp.asarray(t) for t in tables),
    )


def solution(mesh):
    return jax.shard_map(
        on_device,
        mesh=mesh,
        in_specs=(
            P("seq", "ch"),
            P("seq", "ch"),
            P("seq", "ch"),
            P("seq", "ch"),
            P("ch"),
            P("ch", "seq"),
            P("seq", "ch"),
        ),
        out_specs=(P("seq", "ch"), P("seq", "ch"), P("seq", "ch"), P("seq", "ch"), P("ch", "seq")),
        check_vma=False,
    )
```

time: 131 us -> 107 us (0.82)
  Pallas kernels: 109 us -> 92.4 us
  matrix products: 5.7 us -> 0 us
    pallas_call x2 -> x1, Pallas kernels: 109 us -> 92.4 us  [on_device(): pl.pallas_call(whole, out_shape=(shape((rows, chans), BF16), shape((rows,...]
    dot_general x12 -> x0, matrix products: 5.7 us -> none  [the longest x3 2.02 us: inverse(): jnp.einsum('kcn,nm->kcm', jnp.concatenate([re, im], -1), back, precision=...]
    unnamed x37 -> x27, local copies, waits for them, and re-layouts: 13.5 us -> 13.6 us
where the time goes in v3:
time: 107 us
  Pallas kernels  92.4 us (86%)
  local copies, waits for them, and re-layouts  13.6 us (13%)
    pallas_call x1, Pallas kernels, on_device(): pl.pallas_call(whole, out_shape=(shape((rows, chans), BF16), shape((rows,...  92.4 us
    unnamed x27, local copies, waits for them, and re-layouts  13.6 us

profile of v3, /device:TPU:1, one launch (start us, length us, event | category | flops | bytes accessed | tf_op | source)
XLA Modules:
  0.0 106.7 jit_solution(714454006537472366)
XLA Ops:
  0.6 0.0 copy-start
  0.6 1.0 copy-done
  1.7 0.0 copy-start.1
  1.7 1.0 copy-done.1
  2.7 0.0 copy-start.2
  2.7 1.0 copy-done.2
  3.8 0.0 copy-start.3
  3.8 1.0 copy-done.3
  4.7 0.0 copy-start.4
  4.7 0.9 copy-done.4
  5.7 0.0 copy-start.5
  5.7 0.9 copy-done.5
  6.6 0.0 copy-start.6
  6.6 0.9 copy-done.6
  7.5 0.0 copy-start.7
  7.5 0.9 copy-done.7
  8.4 0.0 copy-start.8
  8.4 0.9 copy-done.8
  9.3 0.0 copy-start.9
  9.3 0.9 copy-done.9
  10.2 0.0 copy-start.10
  10.2 0.7 copy-done.10
  10.9 92.4 %whole.1 = (bf16[128,512]{1,0:T(8,128)(2,1)S(1)}, bf16[128,512]{1,0:T(8,128)(2,1)S(1)}, bf16[128,512]{1,0:T(8,128)(2,1)S(1)}, f32[128,512]{1,0:T(8,128)S(1)}, f32[512,128]{1,0:T(8,128)S(1)}) custom-call(bf16[128,512]{1,0:T(8,128)(2,1)S(1)} %copy-done.5, bf16[128,512]{1,0:T(8,128)(2,1)S(1)} %copy-done.6, bf16[128,512]{1,0:T(8,128)(2,1)S(1)} %copy-done.7, ...), custom_call_target="tpu_custom_call" | custom-call | tf_op jit(solution)/shard_map/whole/pallas_call | solution.py:501
  103.3 0.7 copy.21
  104.0 0.7 copy.22
  104.6 0.7 copy.23
  105.3 0.7 copy.24
  106.0 0.7 copy.25
Async XLA Ops:
  0.6 1.0 copy-start
  1.7 1.0 copy-start.1
  2.7 1.0 copy-start.2
  3.8 1.0 copy-start.3
  4.7 0.9 copy-start.4
  5.7 0.9 copy-start.5
  6.6 0.9 copy-start.6
  7.5 0.9 copy-start.7
  8.4 0.9 copy-start.8
  9.3 0.9 copy-start.9
  10.2 0.7 copy-start.10

commit v4 on v3

--- a/solution.py
+++ b/solution.py
@@ -32,13 +32,8 @@
     ahead = np.block([[cos, -sin], [sin, cos]])
     back = np.block([[cos, sin], [-sin, cos]])
 
-    def pair(m):
-        high = np.asarray(m, np.float32).astype(BF16)
-        low = (m - high.astype(np.float64)).astype(BF16)
-        return np.stack([high, low])
-
-    turns = np.stack([np.cos(twist), np.sin(twist)]).astype(np.float32)
-    return pair(outer), pair(outer_back), np.concatenate([pair(ahead), pair(back)]), turns
+    turns = np.stack([np.cos(twist), np.sin(twist)])
+    return tuple(np.asarray(m, np.float32) for m in (outer, outer_back, ahead, back, turns))
 
 
 def halves(x):
@@ -55,9 +50,9 @@
     return dot(const[0], high) + dot(const[0], low) + dot(const[1], high)
 
 
-def dot_const_right(x, const, at):
+def dot_const_right(x, const):
     high, low = halves(x)
-    return dot(high, const[at]) + dot(low, const[at]) + dot(high, const[at + 1])
+    return dot(high, const[0]) + dot(low, const[0]) + dot(high, const[1])
 
 
 def forward(signals, outer, inner, turns):
@@ -70,13 +65,13 @@
         part = y[:, 128 * i : 128 * i + 128]
         re, im = part[:264], jnp.concatenate([rest, part[264:], rest], axis=0)
         rows.append(jnp.concatenate([re * cos + im * sin, im * cos - re * sin], axis=1))
-    z = dot_const_right(jnp.concatenate(rows, axis=0), inner, 0)
+    z = dot_const_right(jnp.concatenate(rows, axis=0), inner)
     return [(z[528 * i : 528 * i + 528, :128], z[528 * i : 528 * i + 528, 128:]) for i in range(len(signals))]
 
 
-def inverse(spectra, outer_back, inner, turns):
+def inverse(spectra, outer_back, inner_back, turns):
     z = jnp.concatenate([jnp.concatenate(pair, axis=1) for pair in spectra], axis=0)
-    z = dot_const_right(z, inner, 2)
+    z = dot_const_right(z, inner_back)
     cos, sin = turns[0], turns[1]
     columns = []
     for i in range(2 * len(spectra)):
@@ -182,39 +177,38 @@
     yield
 
 
-def ring_z(wire, buf, x, z, k, across):
-    def ref(far, *part):
-        return buf.at[(lax.rem(z + far + NZ, NZ) * 2 + k, *part)]
+def ring_z(wire, buf, x, z, k):
+    half = buf.shape[1] // 2
+    low, high, full = (0, half), (half, half), (0, 2 * half)
+
+    def ref(far, part):
+        return buf.at[lax.rem(z + far + NZ, NZ) * 2 + k, pl.ds(*part)]
 
     def send(far, part, step):
         r = ref(far, part)
         return wire.go(r, r, {"seq": place(x, z + step, k)})
 
-    def share(far, *part):
-        r = ref(far, *part)
+    def share(far):
+        r = ref(far, full)
         return wire.go(r, r, {"seq": place(x, z, 1 - k)})
 
-    other = 1 - x
-    right, left = send(0, x, 1), send(0, x, -1)
-    siblings = [share(0, x)]
-    yield
-    across.wait_recv()
-    right2, left2 = send(0, other, 1), send(0, other, -1)
-    siblings.append(share(0, other))
+    right, left = send(0, low, 1), send(0, high, -1)
+    right2, left2 = send(0, high, 1), send(0, low, -1)
+    siblings = [share(0)]
     yield
     for j in (1, 2, 3):
         right.wait_recv()
-        right = send(-j, x, 1)
+        right = send(-j, low, 1)
         left.wait_recv()
-        left = send(j, x, -1) if j < 3 else None
+        left = send(j, high, -1)
         right2.wait_recv()
-        right2 = send(-j, other, 1) if j < 3 else None
+        right2 = send(-j, high, 1) if j < 3 else None
         left2.wait_recv()
-        left2 = send(j, other, -1)
+        left2 = send(j, low, -1) if j < 3 else None
         siblings += [share(-j), share(j)]
         yield
     right.wait_recv()
-    left2.wait_recv()
+    left.wait_recv()
     siblings.append(share(4))
     yield
     for copy in siblings:
@@ -298,12 +292,14 @@
 
 
 def whole(
-    q_hbm, k_hbm, v_hbm, f_hbm, r_hbm, w_hbm, c_hbm, outer_hbm, back_hbm, inner_hbm, turns_hbm,
-    gq_out, gk_out, gv_out, gf_out, gw_out,
-    q_ref, k_ref, v_ref, f_ref, r_ref, outer, back, inner, turns,
-    wbuf, cbuf, tall, gbuf, gg_ref, rate_ref,
-    in_src, in_dst, gm_src, gm_dst, home_src, home_dst, gated_ref, half_src, half_dst,
-    load_sem, wire_send, wire_recv, swap_send, swap_recv,
+    q_hbm, k_hbm, v_hbm, f_hbm, r_hbm, w_hbm, c_hbm,
+    outer_hbm, outer_back_hbm, inner_hbm, inner_back_hbm, turns_hbm,
+    gq_hbm, gk_hbm, gv_hbm, gf_hbm, gw_hbm,
+    q_ref, k_ref, v_ref, f_ref, r_ref, outer_ref, outer_back_ref, inner_ref, inner_back_ref, turns,
+    gq_out, gk_out, gv_out, gf_out, gw_out, outer, outer_back, inner, inner_back,
+    wbuf, cbuf, tall, gbuf, rate_ref,
+    in_src, in_dst, gm_src, gm_dst, home_src, home_dst, qt_ref, half_src, half_dst,
+    load_sem, store_sem, wire_send, wire_recv, swap_send, swap_recv,
 ):
     me, ch = lax.axis_index("seq"), lax.axis_index("ch")
     x, z, k = me // 16, lax.rem(me // 2, NZ), lax.rem(me, 2)
@@ -324,9 +320,10 @@
                 (f_hbm, f_ref),
                 (q_hbm, q_ref),
                 (r_hbm, r_ref),
-                (outer_hbm, outer),
-                (back_hbm, back),
-                (inner_hbm, inner),
+                (outer_hbm, outer_ref),
+                (outer_back_hbm, outer_back_ref),
+                (inner_hbm, inner_ref),
+                (inner_back_hbm, inner_back_ref),
                 (turns_hbm, turns),
             )
         )
@@ -368,7 +365,11 @@
 
     in_src[:, 0:16] = pack(turned(k_ref[...].astype(F32) * v_ref[...].astype(F32)), 2.0**25)
     in_src[:, 16:32] = pack(turned(f_ref[...]), 2.0**28)
-    in_src[:, 32:48] = turned(q_ref[...].astype(F32)).astype(BF16)
+    qt_ref[...] = q_ref[...].astype(F32).T
+    for wide_const, const in (
+        (outer_ref, outer), (outer_back_ref, outer_back), (inner_ref, inner), (inner_back_ref, inner_back)
+    ):
+        const[0], const[1] = halves(wide_const[...])
     rate_ref[...] = jnp.broadcast_to(r_ref[...], (rows, chans)).T
     env = envelope_of(r_ref[...], me, rows)
     own_rates = rate_ref[pl.ds(me * fine, fine), :]
@@ -387,89 +388,86 @@
     advance(weights)
     wide = gather_ch(wire, cbuf, y, xl)
     advance(wide)
+    def swap(i, src, dst):
+        return Swap(src, dst, swap_send.at[i], swap_recv.at[i], me)
+
+    stores = []
+
+    def store(src, dst):
+        copy = pltpu.make_async_copy(src, dst, store_sem.at[len(stores)])
+        copy.start()
+        stores.append(copy)
+
+    early = swap(0, in_src, in_dst)
+    late = swap(1, gm_src, gm_dst)
+    homes = [swap(2 + i, home_src.at[i], home_dst.at[i]) for i in range(3)]
+
+    early.start()
+    advance(weights, 2)
+    advance(wide)
+    advance(weights)
+    advance(wide)
     base = len(wire.made)
     for i, to in enumerate(targets):
         src = cbuf.at[ch, :, pl.ds(i * 128, 128)]
         wire.go(src, tall.at[keeper, lax.rem(me, 4)], to, base + lax.rem(me, 4))
-
-    def swap(i, src, dst):
-        return Swap(src, dst, swap_send.at[i], swap_recv.at[i], me)
-
-    early = swap(0, in_src, in_dst)
-    late = swap(1, gm_src, gm_dst)
-    homes = [swap(2 + i, home_src.at[i], home_dst.at[i]) for i in range(3)]
-
-    early.start(1, 12)
+    early.wait()
+    product = unpack(in_dst[:, 0:16], 2.0**25)
+    filt = unpack(in_dst[:, 16:32], 2.0**28) * envelope
+    (pr, pi), (fr, fi) = forward([product, filt], outer, inner, turns)
     advance(weights)
-    advance(wide)
-    early.start(12, 22)
+    (mixed,) = inverse([(pr * fr - pi * fi, pr * fi + pi * fr)], outer_back, inner_back, turns)
+    home_src[0] = pack(mixed, 2.0**17)
+    homes[0].start()
     advance(weights)
-    advance(wide)
-    early.start(22, PARTS)
-    advance(weights)
+    finish(wide)
+    finish(weights)
+
+    homes[0].wait()
+    mixed_home = unpack(home_dst[0].reshape(chans, rows), 2.0**17)
+    gbuf[zk] = (qt_ref[...] * mixed_home).astype(BF16)
+    ring = ring_z(wire, gbuf, x, z, k)
+    advance(ring)
     for j in range(4):
         pltpu.make_async_copy(tall.at[0, 0], tall.at[0, 0], wire_recv.at[base + j]).wait()
     high = gather_ch(wire, tall, y, xl)
     advance(high)
-    advance(weights)
-    advance(wide)
-    advance(high)
-    advance(weights)
-    advance(high)
-
-    early.wait()
-    product = unpack(in_dst[:, 0:16], 2.0**25)
-    filt = unpack(in_dst[:, 16:32], 2.0**28) * envelope
-    (pr, pi), (fr, fi) = forward([product, filt], outer, inner, turns)
-    (mixed,) = inverse([(pr * fr - pi * fi, pr * fi + pi * fr)], back, inner, turns)
-    gated_ref[...] = (in_dst[:, 32:48].astype(F32) * mixed).astype(BF16)
-    across = wire.go(
-        gated_ref.at[pl.ds(16 * (1 - x), 16)], gbuf.at[zk, x], {"seq": place(1 - x, z, k)}
-    )
-    gbuf[zk, x] = gated_ref[pl.ds(16 * x, 16)]
-    ring = ring_z(wire, gbuf, x, z, k, across)
-    advance(ring)
-    home_src[0] = pack(mixed, 2.0**17)
-    homes[0].start()
-
-    finish(weights)
-    finish(wide)
     total = jnp.zeros((rows, chans), F32)
     for h in range(WIDE):
         part = jnp.concatenate([wbuf[4 * h + i] for i in range(4)], axis=1)
         total += lax.dot_general(
             cbuf[h], part, (((1,), (1,)), ((), ())), preferred_element_type=F32
         )
-    gg_ref[...] = total
     gm_src[...] = pack(turned(q_ref[...].astype(F32) * total), 2.0**17)
     late.start()
-    advance(ring, 2)
-    finish(high)
+    advance(ring)
+    advance(high)
+    gq_out[...] = (mixed_home.T * total).astype(BF16)
+    store(gq_out, gq_hbm)
+    advance(ring)
+    advance(high)
     late.wait()
     grad = unpack(gm_dst[...], 2.0**17)
     ((gr, gi),) = forward([grad], outer, inner, turns)
     advance(ring)
     back_product, back_taps = inverse(
         [(gr * fr + gi * fi, gi * fr - gr * fi), (gr * pr + gi * pi, gi * pr - gr * pi)],
-        back, inner, turns,
+        outer_back, inner_back, turns,
     )
     home_src[1] = pack(back_product, 2.0**8)
     homes[1].start()
     home_src[2] = pack(back_taps, 1.0)
     homes[2].start()
     finish(ring)
+    finish(high)
 
     total = jnp.zeros((chans, 256), F32)
     for a in range(4):
-        left, right = [], []
-        for j in range(4):
-            block = 4 * a + j
-            left.append(
-                jnp.concatenate([gbuf[:, i, block].reshape(256, 128) for i in range(2)], axis=0)
-            )
-            right.append(
-                jnp.concatenate([tall[(4 * i + a + 1 + j) % WIDE, j] for i in range(2)], axis=1)
-            )
+        left = [gbuf[4 * a + j] for j in range(4)]
+        right = [
+            jnp.concatenate([tall[(4 * i + a + 1 + j) % WIDE, j] for i in range(2)], axis=1)
+            for j in range(4)
+        ]
         total += dot(jnp.concatenate(left, axis=1), jnp.concatenate(right, axis=0))
     mine = jnp.where(x == 0, total[:, :128], total[:, 128:])
     theirs = jnp.where(x == 0, total[:, 128:], total[:, :128])
@@ -480,14 +478,32 @@
         homes[i].wait()
         return unpack(home_dst[i].reshape(chans, rows), scale).T
 
-    gq_out[...] = (arrived(0, 2.0**17) * gg_ref[...]).astype(BF16)
     grad_product = arrived(1, 2.0**8)
     gk_out[...] = (grad_product * v_ref[...].astype(F32)).astype(BF16)
+    store(gk_out, gk_hbm)
     gv_out[...] = (grad_product * k_ref[...].astype(F32)).astype(BF16)
+    store(gv_out, gv_hbm)
     gf_out[...] = arrived(2, 1.0) * env
+    store(gf_out, gf_hbm)
     last.wait_recv()
     gw_out[...] = mine + unpack(half_dst[...], 1.0)
+    store(gw_out, gw_hbm)
+    for copy in stores:
+        copy.wait()
     wire.drain()
+
+
+def hand_over(*refs):
+    src, dst, held, load_sem, store_sem = refs[:5], refs[5:10], refs[10:15], refs[15], refs[16]
+    loads = [pltpu.make_async_copy(src[i], held[i], load_sem.at[i]) for i in range(5)]
+    stores = [pltpu.make_async_copy(held[i], dst[i], store_sem.at[i]) for i in range(5)]
+    for load in loads:
+        load.start()
+    for load, copy in zip(loads, stores):
+        load.wait()
+        copy.start()
+    for copy in stores:
+        copy.wait()
 
 
 def on_device(query, key, value, filter_raw, rates, out_weight, cotangent):
@@ -498,17 +514,19 @@
     shape = jax.ShapeDtypeStruct
     block = pltpu.VMEM((rows, chans), BF16)
     piece = (PARTS, fine, rows)
-    return pl.pallas_call(
+    out_shape = (
+        shape((rows, chans), BF16),
+        shape((rows, chans), BF16),
+        shape((rows, chans), BF16),
+        shape((rows, chans), F32),
+        shape(out_weight.shape, F32),
+    )
+    anywhere = pl.BlockSpec(memory_space=pl.ANY)
+    results = pl.pallas_call(
         whole,
-        out_shape=(
-            shape((rows, chans), BF16),
-            shape((rows, chans), BF16),
-            shape((rows, chans), BF16),
-            shape((rows, chans), F32),
-            shape(out_weight.shape, F32),
-        ),
-        in_specs=[pl.BlockSpec(memory_space=pl.ANY)] * 11,
-        out_specs=(pl.BlockSpec(memory_space=pltpu.VMEM),) * 5,
+        out_shape=out_shape,
+        in_specs=[anywhere] * 12,
+        out_specs=(anywhere,) * 5,
         scratch_shapes=[
             block,
             block,
@@ -516,35 +534,47 @@
             pltpu.VMEM((rows, chans), F32),
             pltpu.VMEM((1, chans), F32),
             *(pltpu.VMEM(t.shape, t.dtype) for t in tables),
+            *(pltpu.VMEM(o.shape, o.dtype) for o in out_shape),
+            *(pltpu.VMEM((2, *t.shape), BF16) for t in tables[:4]),
             pltpu.VMEM((PARTS, chans, columns), BF16),
             pltpu.VMEM((WIDE, rows, chans), BF16),
             pltpu.VMEM((WIDE, 4, rows, columns), BF16),
-            pltpu.VMEM((16, 2, 16, fine, rows), BF16),
-            pltpu.VMEM((rows, chans), F32),
+            pltpu.VMEM((16, chans, rows), BF16),
             pltpu.VMEM((chans, rows), F32),
-            pltpu.VMEM((PARTS, 3 * fine, rows), BF16),
-            pltpu.VMEM((PARTS, 3 * fine, rows), BF16),
+            pltpu.VMEM((PARTS, 2 * fine, rows), BF16),
+            pltpu.VMEM((PARTS, 2 * fine, rows), BF16),
             pltpu.VMEM(piece, BF16),
             pltpu.VMEM(piece, BF16),
             pltpu.VMEM((3, *piece), BF16),
             pltpu.VMEM((3, *piece), BF16),
-            pltpu.VMEM(piece, BF16),
+            pltpu.VMEM((chans, rows), F32),
             pltpu.VMEM((chans, columns), BF16),
             pltpu.VMEM((chans, columns), BF16),
-            pltpu.SemaphoreType.DMA((11,)),
+            pltpu.SemaphoreType.DMA((12,)),
+            pltpu.SemaphoreType.DMA((5,)),
             pltpu.SemaphoreType.DMA((128,)),
             pltpu.SemaphoreType.DMA((128,)),
             pltpu.SemaphoreType.DMA((5, PARTS)),
             pltpu.SemaphoreType.DMA((5, PARTS)),
         ],
         compiler_params=pltpu.CompilerParams(
-            collective_id=0, has_side_effects=True, vmem_limit_bytes=48 * 2**20
+            collective_id=0, has_side_effects=True, vmem_limit_bytes=63 * 2**20
         ),
         name="whole",
     )(
         query, key, value, filter_raw, rates.reshape(1, chans), out_weight, cotangent,
         *(jnp.asarray(t) for t in tables),
     )
+    return pl.pallas_call(
+        hand_over,
+        out_shape=out_shape,
+        in_specs=[anywhere] * 5,
+        out_specs=(anywhere,) * 5,
+        scratch_shapes=[pltpu.VMEM(o.shape, o.dtype) for o in out_shape]
+        + [pltpu.SemaphoreType.DMA((5,)), pltpu.SemaphoreType.DMA((5,))],
+        compiler_params=pltpu.CompilerParams(vmem_limit_bytes=63 * 2**20),
+        name="hand_over",
+    )(*results)
 
 
 def solution(mesh):

time: 107 us -> 85.4 us (0.80)
  local copies, waits for them, and re-layouts: 13.6 us -> 0 us
  Pallas kernels: 92.4 us -> 84.6 us
    unnamed x27 -> x0, local copies, waits for them, and re-layouts: 13.6 us -> none
    pallas_call x1 -> x2, Pallas kernels: 92.4 us -> 84.6 us  [the longest x1 82.6 us: on_device(): pl.pallas_call(whole, out_shape=out_shape, in_specs=[anywhere] * 12, out_...]
where the time goes in v4:
time: 85.4 us; the launch traced here: 85.2 us
  Pallas kernels  84.6 us (99%)
    pallas_call x1, Pallas kernels, on_device(): pl.pallas_call(whole, out_shape=out_shape, in_specs=[anywhere] * 12, out_...  82.6 us
    pallas_call x1, Pallas kernels, on_device(): pl.pallas_call(hand_over, out_shape=out_shape, in_specs=[anywhere] * 5, o...  2.02 us

profile of v4, /device:TPU:1, one launch (start us, length us, event | category | flops | bytes accessed | tf_op | source)
XLA Modules:
  0.0 85.2 jit_solution(5598693069202226390)
XLA Ops:
  0.6 82.6 %whole.1 = (bf16[128,512]{1,0:T(8,128)(2,1)}, bf16[128,512]{1,0:T(8,128)(2,1)}, bf16[128,512]{1,0:T(8,128)(2,1)}, f32[128,512]{1,0:T(8,128)}, f32[512,128]{1,0:T(8,128)}) custom-call(bf16[128,512]{1,0:T(8,128)(2,1)} %q_hbm.1, bf16[128,512]{1,0:T(8,128)(2,1)} %k_hbm.1, bf16[128,512]{1,0:T(8,128)(2,1)} %v_hbm.1, f32[128,512]{1,0:T(8,128)} %f_hbm.1, ...), custom_call_target="tpu_custom_call" | custom-call | tf_op jit(solution)/shard_map/whole/pallas_call | solution.py:525
  83.2 2.0 %hand_over.1 = (bf16[128,512]{1,0:T(8,128)(2,1)}, bf16[128,512]{1,0:T(8,128)(2,1)}, bf16[128,512]{1,0:T(8,128)(2,1)}, f32[128,512]{1,0:T(8,128)}, f32[512,128]{1,0:T(8,128)}) custom-call(bf16[128,512]{1,0:T(8,128)(2,1)} %get-tuple-element.10.refs_0_, bf16[128,512]{1,0:T(8,128)(2,1)} %get-tuple-element.11.refs_1_, ...), custom_call_target="tpu_custom_call" | custom-call | tf_op jit(solution)/shard_map/hand_over/pallas_call | solution.py:568

commit v5 on v4

--- a/solution.py
+++ b/solution.py
@@ -123,8 +123,8 @@
 
 def gather_seq(wire, buf, x, z, k):
     rows = buf.shape[1]
-    half, quarter = rows // 2, rows // 4
-    low, high, full = (0, half), (half, half), (0, rows)
+    cut = rows * 4 // 8
+    low, high, full = (0, cut), (cut, rows - cut), (0, rows)
 
     def send(src_x, src_z, part, dst):
         ref = buf.at[place(src_x, src_z, k), pl.ds(*part)]
@@ -132,45 +132,51 @@
 
     sib, par, right, left = (x, z, 1 - k), (1 - x, z, k), (x, z + 1, k), (x, z - 1, k)
     other = 1 - x
-    siblings, across = [], []
-    r = send(x, z, full, right)
-    l = send(x, z, full, left)
-    first = send(x, z, full, par)
-    siblings.append(send(x, z, full, sib))
+    right_high, left_high = send(x, z, high, right), send(x, z, high, left)
+    first = send(x, z, low, par)
+    right_low, left_low = send(x, z, low, right), send(x, z, low, left)
+    across = [(z, send(x, z, high, par))]
+    siblings = [send(x, z, full, sib)]
     yield
     first.wait_recv()
-    pr = send(other, z, low, right)
-    pl_ = send(other, z, low, left)
-    siblings.append(send(other, z, full, sib))
+    right_other, left_other = send(other, z, low, right), send(other, z, low, left)
     yield
     for j in (1, 2, 3):
-        r.wait_recv()
-        r = send(x, z - j, full if j < 3 else low, right)
-        across.append((z - j, send(x, z - j, high, par)))
+        right_high.wait_recv()
+        right_high = send(x, z - j, high, right) if j < 3 else None
+        behind = send(x, z - j, high, par)
+        left_high.wait_recv()
+        left_high = send(x, z + j, high, left)
+        ahead = send(x, z + j, high, par)
+        right_low.wait_recv()
+        right_low = send(x, z - j, low, right)
         siblings.append(send(x, z - j, full, sib))
-        l.wait_recv()
-        l = send(x, z + j, full if j < 3 else high, left)
-        across.append((z + j, send(x, z + j, high, par)))
+        left_low.wait_recv()
+        left_low = send(x, z + j, low, left) if j < 3 else None
         siblings.append(send(x, z + j, full, sib))
-        pr.wait_recv()
-        pr = send(other, z - j, low if j < 3 else (0, quarter), right)
-        siblings.append(send(other, z - j, low, sib))
-        pl_.wait_recv()
-        pl_ = send(other, z + j, low if j < 3 else (quarter, quarter), left)
-        siblings.append(send(other, z + j, low, sib))
+        right_other.wait_recv()
+        right_other = send(other, z - j, low if j < 3 else (0, cut // 2), right)
+        left_other.wait_recv()
+        left_other = send(other, z + j, low if j < 3 else (cut // 2, cut // 2), left)
+        for far, copy in across:
+            copy.wait_recv()
+            siblings.append(send(other, far, full, sib))
+        across = [(z - j, behind), (z + j, ahead)]
         yield
-    l.wait_recv()
-    across.append((z + 4, send(x, z + 4, high, par)))
+    left_high.wait_recv()
+    last = send(x, z + 4, high, par)
     siblings.append(send(x, z + 4, high, sib))
-    r.wait_recv()
+    right_low.wait_recv()
     siblings.append(send(x, z + 4, low, sib))
-    pr.wait_recv()
-    pl_.wait_recv()
-    siblings.append(send(other, z + 4, low, sib))
-    yield
     for far, copy in across:
         copy.wait_recv()
-        siblings.append(send(other, far, high, sib))
+        siblings.append(send(other, far, full, sib))
+    right_other.wait_recv()
+    left_other.wait_recv()
+    siblings.append(send(other, z + 4, low, sib))
+    yield
+    last.wait_recv()
+    siblings.append(send(other, z + 4, high, sib))
     yield
     for copy in siblings:
         copy.wait_recv()
@@ -263,8 +269,8 @@
         return pltpu.make_async_remote_copy(
             src_ref=self.src.at[target],
             dst_ref=self.dst.at[self.me],
-            send_sem=self.send.at[d],
-            recv_sem=self.recv.at[d],
+            send_sem=self.send,
+            recv_sem=self.recv,
             device_id={"seq": target},
             device_id_type=MESH,
         )
@@ -278,9 +284,9 @@
             self.dst[self.me] = self.src[self.me]
 
     def wait(self):
-        @pl.loop(1, PARTS)
-        def _(d):
-            self.copy(d).wait()
+        for ref, sem in ((self.dst, self.recv), (self.src, self.send)):
+            all_pieces = ref.at[pl.ds(0, PARTS - 1)]
+            pltpu.make_async_copy(all_pieces, all_pieces, sem).wait()
 
 
 def envelope_of(rates, me, rows):
@@ -357,14 +363,40 @@
     for to in greeted:
         pl.semaphore_signal(barrier, inc=1, device_id=to, device_id_type=MESH)
 
-    for load in loads:
-        load.wait()
 
     def turned(value):
         return value.T.reshape(PARTS, fine, rows)
 
+    def swap(i, src, dst):
+        return Swap(src, dst, swap_send.at[i], swap_recv.at[i], me)
+
+    stores = []
+
+    def store(src, dst):
+        copy = pltpu.make_async_copy(src, dst, store_sem.at[len(stores)])
+        copy.start()
+        stores.append(copy)
+
+    early = swap(0, in_src, in_dst)
+    late = swap(1, gm_src, gm_dst)
+    homes = [swap(2 + i, home_src.at[i], home_dst.at[i]) for i in range(3)]
+
+    loads[0].wait()
+    loads[1].wait()
+    pl.semaphore_wait(barrier, PARTS - 1 + len(greeted))
+    weights = gather_seq(wire, wbuf, x, z, k)
+    advance(weights)
+    wide = gather_ch(wire, cbuf, y, xl)
+    advance(wide)
+    for load in loads[2:5]:
+        load.wait()
     in_src[:, 0:16] = pack(turned(k_ref[...].astype(F32) * v_ref[...].astype(F32)), 2.0**25)
     in_src[:, 16:32] = pack(turned(f_ref[...]), 2.0**28)
+    early.start()
+    advance(weights)
+    advance(wide)
+    for load in loads[5:]:
+        load.wait()
     qt_ref[...] = q_ref[...].astype(F32).T
     for wide_const, const in (
         (outer_ref, outer), (outer_back_ref, outer_back), (inner_ref, inner), (inner_back_ref, inner_back)
@@ -382,52 +414,30 @@
             for block in range(PARTS)
         ]
     )
-    pl.semaphore_wait(barrier, PARTS - 1 + len(greeted))
-
-    weights = gather_seq(wire, wbuf, x, z, k)
     advance(weights)
-    wide = gather_ch(wire, cbuf, y, xl)
-    advance(wide)
-    def swap(i, src, dst):
-        return Swap(src, dst, swap_send.at[i], swap_recv.at[i], me)
-
-    stores = []
-
-    def store(src, dst):
-        copy = pltpu.make_async_copy(src, dst, store_sem.at[len(stores)])
-        copy.start()
-        stores.append(copy)
-
-    early = swap(0, in_src, in_dst)
-    late = swap(1, gm_src, gm_dst)
-    homes = [swap(2 + i, home_src.at[i], home_dst.at[i]) for i in range(3)]
-
-    early.start()
-    advance(weights, 2)
-    advance(wide)
     advance(weights)
-    advance(wide)
-    base = len(wire.made)
-    for i, to in enumerate(targets):
-        src = cbuf.at[ch, :, pl.ds(i * 128, 128)]
-        wire.go(src, tall.at[keeper, lax.rem(me, 4)], to, base + lax.rem(me, 4))
     early.wait()
     product = unpack(in_dst[:, 0:16], 2.0**25)
     filt = unpack(in_dst[:, 16:32], 2.0**28) * envelope
     (pr, pi), (fr, fi) = forward([product, filt], outer, inner, turns)
     advance(weights)
+    advance(wide)
     (mixed,) = inverse([(pr * fr - pi * fi, pr * fi + pi * fr)], outer_back, inner_back, turns)
     home_src[0] = pack(mixed, 2.0**17)
     homes[0].start()
+    base = len(wire.made)
+    for i, to in enumerate(targets):
+        src = cbuf.at[ch, :, pl.ds(i * 128, 128)]
+        wire.go(src, tall.at[keeper, lax.rem(me, 4)], to, base + lax.rem(me, 4))
     advance(weights)
     finish(wide)
-    finish(weights)
-
+    advance(weights)
     homes[0].wait()
     mixed_home = unpack(home_dst[0].reshape(chans, rows), 2.0**17)
     gbuf[zk] = (qt_ref[...] * mixed_home).astype(BF16)
     ring = ring_z(wire, gbuf, x, z, k)
     advance(ring)
+    finish(weights)
     for j in range(4):
         pltpu.make_async_copy(tall.at[0, 0], tall.at[0, 0], wire_recv.at[base + j]).wait()
     high = gather_ch(wire, tall, y, xl)
@@ -461,18 +471,18 @@
     finish(ring)
     finish(high)
 
-    total = jnp.zeros((chans, 256), F32)
-    for a in range(4):
-        left = [gbuf[4 * a + j] for j in range(4)]
-        right = [
-            jnp.concatenate([tall[(4 * i + a + 1 + j) % WIDE, j] for i in range(2)], axis=1)
-            for j in range(4)
-        ]
-        total += dot(jnp.concatenate(left, axis=1), jnp.concatenate(right, axis=0))
-    mine = jnp.where(x == 0, total[:, :128], total[:, 128:])
-    theirs = jnp.where(x == 0, total[:, 128:], total[:, :128])
-    half_src[...] = pack(theirs, 1.0)
+    def columns_of(half):
+        total = jnp.zeros((chans, 128), F32)
+        for a in range(4):
+            left = jnp.concatenate([gbuf[4 * a + j] for j in range(4)], axis=1)
+            slots = [lax.rem(4 * half + a + 1 + j, WIDE) for j in range(4)]
+            right = jnp.concatenate([tall[slots[j], j] for j in range(4)], axis=0)
+            total += dot(left, right)
+        return total
+
+    half_src[...] = pack(columns_of(1 - x), 1.0)
     last = wire.go(half_src, half_dst, {"seq": place(1 - x, z, k)})
+    mine = columns_of(x)
 
     def arrived(i, scale):
         homes[i].wait()
@@ -552,10 +562,10 @@
             pltpu.VMEM((chans, columns), BF16),
             pltpu.SemaphoreType.DMA((12,)),
             pltpu.SemaphoreType.DMA((5,)),
-            pltpu.SemaphoreType.DMA((128,)),
-            pltpu.SemaphoreType.DMA((128,)),
-            pltpu.SemaphoreType.DMA((5, PARTS)),
-            pltpu.SemaphoreType.DMA((5, PARTS)),
+            pltpu.SemaphoreType.DMA((94,)),
+            pltpu.SemaphoreType.DMA((94,)),
+            pltpu.SemaphoreType.DMA((5,)),
+            pltpu.SemaphoreType.DMA((5,)),
         ],
         compiler_params=pltpu.CompilerParams(
             collective_id=0, has_side_effects=True, vmem_limit_bytes=63 * 2**20

time: 85.4 us -> 78.2 us (0.916)
  Pallas kernels: 84.6 us -> 77.4 us
    pallas_call x1, Pallas kernels: 82.6 us -> 75.4 us  [on_device(): pl.pallas_call(whole, out_shape=out_shape, in_specs=[anywhere] * 12, out_...]
where the time goes in v5:
time: 78.2 us; the launch traced here: 78 us
  Pallas kernels  77.4 us (99%)
    pallas_call x1, Pallas kernels, on_device(): pl.pallas_call(whole, out_shape=out_shape, in_specs=[anywhere] * 12, out_...  75.4 us
    pallas_call x1, Pallas kernels, on_device(): pl.pallas_call(hand_over, out_shape=out_shape, in_specs=[anywhere] * 5, o...  2.02 us

profile of v5, /device:TPU:1, one launch (start us, length us, event | category | flops | bytes accessed | tf_op | source)
XLA Modules:
  0.0 78.0 jit_solution(5770635166974599447)
XLA Ops:
  0.6 75.4 %whole.1 = (bf16[128,512]{1,0:T(8,128)(2,1)}, bf16[128,512]{1,0:T(8,128)(2,1)}, bf16[128,512]{1,0:T(8,128)(2,1)}, f32[128,512]{1,0:T(8,128)}, f32[512,128]{1,0:T(8,128)}) custom-call(bf16[128,512]{1,0:T(8,128)(2,1)} %q_hbm.1, bf16[128,512]{1,0:T(8,128)(2,1)} %k_hbm.1, bf16[128,512]{1,0:T(8,128)(2,1)} %v_hbm.1, f32[128,512]{1,0:T(8,128)} %f_hbm.1, ...), custom_call_target="tpu_custom_call" | custom-call | tf_op jit(solution)/shard_map/whole/pallas_call | solution.py:535
  76.0 2.0 %hand_over.1 = (bf16[128,512]{1,0:T(8,128)(2,1)}, bf16[128,512]{1,0:T(8,128)(2,1)}, bf16[128,512]{1,0:T(8,128)(2,1)}, f32[128,512]{1,0:T(8,128)}, f32[512,128]{1,0:T(8,128)}) custom-call(bf16[128,512]{1,0:T(8,128)(2,1)} %get-tuple-element.10.refs_0_, bf16[128,512]{1,0:T(8,128)(2,1)} %get-tuple-element.11.refs_1_, ...), custom_call_target="tpu_custom_call" | custom-call | tf_op jit(solution)/shard_map/hand_over/pallas_call | solution.py:578

commit v6 on v5

--- a/solution.py
+++ b/solution.py
@@ -96,25 +96,34 @@
 
 class Wire:
     def __init__(self, send, recv):
-        self.send, self.recv, self.made = send, recv, []
-
-    def go(self, src, dst, to, there=None):
-        i = len(self.made)
+        self.send, self.recv = send, recv
+        self.used = 0
+        self.groups = []
+
+    def group(self, sent):
+        self.groups.append(sent)
+        return len(self.groups) - 1
+
+    def slot(self, count=1):
+        self.used += count
+        return self.used - count
+
+    def go(self, src, dst, to, group, there=None):
+        i = self.slot() if there is None else there
         copy = pltpu.make_async_remote_copy(
             src_ref=src,
             dst_ref=dst,
-            send_sem=self.send.at[i],
-            recv_sem=self.recv.at[i if there is None else there],
+            send_sem=self.send.at[group],
+            recv_sem=self.recv.at[i],
             device_id=to,
             device_id_type=MESH,
         )
         copy.start()
-        self.made.append(copy)
         return copy
 
     def drain(self):
-        for copy in self.made:
-            copy.wait_send()
+        for i, sent in enumerate(self.groups):
+            pltpu.make_async_copy(sent, sent, self.send.at[i]).wait()
 
 
 def place(x, z, k):
@@ -123,12 +132,15 @@
 
 def gather_seq(wire, buf, x, z, k):
     rows = buf.shape[1]
-    cut = rows * 4 // 8
+    cut = rows * 3 // 8
     low, high, full = (0, cut), (cut, rows - cut), (0, rows)
 
-    def send(src_x, src_z, part, dst):
+    group = wire.group(buf.at[pl.ds(0, 31)])
+    shared = wire.slot()
+
+    def send(src_x, src_z, part, dst, there=None):
         ref = buf.at[place(src_x, src_z, k), pl.ds(*part)]
-        return wire.go(ref, ref, {"seq": place(*dst)})
+        return wire.go(ref, ref, {"seq": place(*dst)}, group, there)
 
     sib, par, right, left = (x, z, 1 - k), (1 - x, z, k), (x, z + 1, k), (x, z - 1, k)
     other = 1 - x
@@ -136,7 +148,7 @@
     first = send(x, z, low, par)
     right_low, left_low = send(x, z, low, right), send(x, z, low, left)
     across = [(z, send(x, z, high, par))]
-    siblings = [send(x, z, full, sib)]
+    send(x, z, full, sib, shared)
     yield
     first.wait_recv()
     right_other, left_other = send(other, z, low, right), send(other, z, low, left)
@@ -150,36 +162,35 @@
         ahead = send(x, z + j, high, par)
         right_low.wait_recv()
         right_low = send(x, z - j, low, right)
-        siblings.append(send(x, z - j, full, sib))
+        send(x, z - j, full, sib, shared)
         left_low.wait_recv()
         left_low = send(x, z + j, low, left) if j < 3 else None
-        siblings.append(send(x, z + j, full, sib))
+        send(x, z + j, full, sib, shared)
         right_other.wait_recv()
         right_other = send(other, z - j, low if j < 3 else (0, cut // 2), right)
         left_other.wait_recv()
         left_other = send(other, z + j, low if j < 3 else (cut // 2, cut // 2), left)
         for far, copy in across:
             copy.wait_recv()
-            siblings.append(send(other, far, full, sib))
+            send(other, far, full, sib, shared)
         across = [(z - j, behind), (z + j, ahead)]
         yield
     left_high.wait_recv()
     last = send(x, z + 4, high, par)
-    siblings.append(send(x, z + 4, high, sib))
+    send(x, z + 4, high, sib, shared)
     right_low.wait_recv()
-    siblings.append(send(x, z + 4, low, sib))
+    send(x, z + 4, low, sib, shared)
     for far, copy in across:
         copy.wait_recv()
-        siblings.append(send(other, far, full, sib))
+        send(other, far, full, sib, shared)
     right_other.wait_recv()
     left_other.wait_recv()
-    siblings.append(send(other, z + 4, low, sib))
+    send(other, z + 4, low, sib, shared)
     yield
     last.wait_recv()
-    siblings.append(send(other, z + 4, high, sib))
-    yield
-    for copy in siblings:
-        copy.wait_recv()
+    send(other, z + 4, high, sib, shared)
+    yield
+    pltpu.make_async_copy(buf.at[pl.ds(0, 16)], buf.at[pl.ds(0, 16)], wire.recv.at[shared]).wait()
     yield
 
 
@@ -187,20 +198,23 @@
     half = buf.shape[1] // 2
     low, high, full = (0, half), (half, half), (0, 2 * half)
 
+    group = wire.group(buf.at[pl.ds(0, 15)])
+    shared = wire.slot()
+
     def ref(far, part):
         return buf.at[lax.rem(z + far + NZ, NZ) * 2 + k, pl.ds(*part)]
 
     def send(far, part, step):
         r = ref(far, part)
-        return wire.go(r, r, {"seq": place(x, z + step, k)})
+        return wire.go(r, r, {"seq": place(x, z + step, k)}, group)
 
     def share(far):
         r = ref(far, full)
-        return wire.go(r, r, {"seq": place(x, z, 1 - k)})
+        wire.go(r, r, {"seq": place(x, z, 1 - k)}, group, shared)
 
     right, left = send(0, low, 1), send(0, high, -1)
     right2, left2 = send(0, high, 1), send(0, low, -1)
-    siblings = [share(0)]
+    share(0)
     yield
     for j in (1, 2, 3):
         right.wait_recv()
@@ -211,23 +225,25 @@
         right2 = send(-j, high, 1) if j < 3 else None
         left2.wait_recv()
         left2 = send(j, low, -1) if j < 3 else None
-        siblings += [share(-j), share(j)]
+        share(-j)
+        share(j)
         yield
     right.wait_recv()
     left.wait_recv()
-    siblings.append(share(4))
-    yield
-    for copy in siblings:
-        copy.wait_recv()
+    share(4)
+    yield
+    pltpu.make_async_copy(buf.at[pl.ds(0, 8)], buf.at[pl.ds(0, 8)], wire.recv.at[shared]).wait()
     yield
 
 
 def gather_ch(wire, buf, y, x):
     half = buf.shape[1] // 2
 
+    group = wire.group(buf.at[pl.ds(0, 7)])
+
     def send(src_y, src_x, part, dst_y, dst_x):
         ref = buf.at[lax.rem(src_y + NY, NY) * 2 + src_x, pl.ds(*part)]
-        return wire.go(ref, ref, {"ch": lax.rem(dst_y + NY, NY) * 2 + dst_x})
+        return wire.go(ref, ref, {"ch": lax.rem(dst_y + NY, NY) * 2 + dst_x}, group)
 
     full, low, high = (0, 2 * half), (0, half), (half, half)
     first = send(y, x, full, y, 1 - x)
@@ -425,10 +441,11 @@
     (mixed,) = inverse([(pr * fr - pi * fi, pr * fi + pi * fr)], outer_back, inner_back, turns)
     home_src[0] = pack(mixed, 2.0**17)
     homes[0].start()
-    base = len(wire.made)
+    base = wire.slot(4)
+    columns_sent = wire.group(tall.at[0])
     for i, to in enumerate(targets):
         src = cbuf.at[ch, :, pl.ds(i * 128, 128)]
-        wire.go(src, tall.at[keeper, lax.rem(me, 4)], to, base + lax.rem(me, 4))
+        wire.go(src, tall.at[keeper, lax.rem(me, 4)], to, columns_sent, base + lax.rem(me, 4))
     advance(weights)
     finish(wide)
     advance(weights)
@@ -481,7 +498,9 @@
         return total
 
     half_src[...] = pack(columns_of(1 - x), 1.0)
-    last = wire.go(half_src, half_dst, {"seq": place(1 - x, z, k)})
+    last = wire.go(
+        half_src, half_dst, {"seq": place(1 - x, z, k)}, wire.group(half_src)
+    )
     mine = columns_of(x)
 
     def arrived(i, scale):
@@ -562,8 +581,8 @@
             pltpu.VMEM((chans, columns), BF16),
             pltpu.SemaphoreType.DMA((12,)),
             pltpu.SemaphoreType.DMA((5,)),
-            pltpu.SemaphoreType.DMA((94,)),
-            pltpu.SemaphoreType.DMA((94,)),
+            pltpu.SemaphoreType.DMA((6,)),
+            pltpu.SemaphoreType.DMA((70,)),
             pltpu.SemaphoreType.DMA((5,)),
             pltpu.SemaphoreType.DMA((5,)),
         ],

time: 78.2 us -> 76.1 us (0.973)
  Pallas kernels: 77.4 us -> 75.3 us
    pallas_call x1, Pallas kernels: 75.4 us -> 73.3 us  [on_device(): pl.pallas_call(whole, out_shape=out_shape, in_specs=[anywhere] * 12, out_...]
where the time goes in v6:
time: 76.1 us; the launch traced here: 76 us
  Pallas kernels  75.3 us (99%)
    pallas_call x1, Pallas kernels, on_device(): pl.pallas_call(whole, out_shape=out_shape, in_specs=[anywhere] * 12, out_...  73.3 us
    pallas_call x1, Pallas kernels, on_device(): pl.pallas_call(hand_over, out_shape=out_shape, in_specs=[anywhere] * 5, o...  2.02 us

profile of v6, /device:TPU:1, one launch (start us, length us, event | category | flops | bytes accessed | tf_op | source)
XLA Modules:
  0.0 76.0 jit_solution(12814642669375420688)
XLA Ops:
  0.6 73.3 %whole.1 = (bf16[128,512]{1,0:T(8,128)(2,1)}, bf16[128,512]{1,0:T(8,128)(2,1)}, bf16[128,512]{1,0:T(8,128)(2,1)}, f32[128,512]{1,0:T(8,128)}, f32[512,128]{1,0:T(8,128)}) custom-call(bf16[128,512]{1,0:T(8,128)(2,1)} %q_hbm.1, bf16[128,512]{1,0:T(8,128)(2,1)} %k_hbm.1, bf16[128,512]{1,0:T(8,128)(2,1)} %v_hbm.1, f32[128,512]{1,0:T(8,128)} %f_hbm.1, ...), custom_call_target="tpu_custom_call" | custom-call | tf_op jit(solution)/shard_map/whole/pallas_call | solution.py:554
  74.0 2.0 %hand_over.1 = (bf16[128,512]{1,0:T(8,128)(2,1)}, bf16[128,512]{1,0:T(8,128)(2,1)}, bf16[128,512]{1,0:T(8,128)(2,1)}, f32[128,512]{1,0:T(8,128)}, f32[512,128]{1,0:T(8,128)}) custom-call(bf16[128,512]{1,0:T(8,128)(2,1)} %get-tuple-element.10.refs_0_, bf16[128,512]{1,0:T(8,128)(2,1)} %get-tuple-element.11.refs_1_, ...), custom_call_target="tpu_custom_call" | custom-call | tf_op jit(solution)/shard_map/hand_over/pallas_call | solution.py:597

commit v7 on v6

--- a/solution.py
+++ b/solution.py
@@ -320,7 +320,7 @@
     q_ref, k_ref, v_ref, f_ref, r_ref, outer_ref, outer_back_ref, inner_ref, inner_back_ref, turns,
     gq_out, gk_out, gv_out, gf_out, gw_out, outer, outer_back, inner, inner_back,
     wbuf, cbuf, tall, gbuf, rate_ref,
-    in_src, in_dst, gm_src, gm_dst, home_src, home_dst, qt_ref, half_src, half_dst,
+    in_src, in_dst, gm_src, gm_dst, home_src, home_dst, pair_src, pair_dst, qt_ref, half_src, half_dst,
     load_sem, store_sem, wire_send, wire_recv, swap_send, swap_recv,
 ):
     me, ch = lax.axis_index("seq"), lax.axis_index("ch")
@@ -395,7 +395,8 @@
 
     early = swap(0, in_src, in_dst)
     late = swap(1, gm_src, gm_dst)
-    homes = [swap(2 + i, home_src.at[i], home_dst.at[i]) for i in range(3)]
+    home = swap(2, home_src, home_dst)
+    pair = swap(3, pair_src, pair_dst)
 
     loads[0].wait()
     loads[1].wait()
@@ -439,8 +440,8 @@
     advance(weights)
     advance(wide)
     (mixed,) = inverse([(pr * fr - pi * fi, pr * fi + pi * fr)], outer_back, inner_back, turns)
-    home_src[0] = pack(mixed, 2.0**17)
-    homes[0].start()
+    home_src[...] = pack(mixed, 2.0**17)
+    home.start()
     base = wire.slot(4)
     columns_sent = wire.group(tall.at[0])
     for i, to in enumerate(targets):
@@ -449,8 +450,8 @@
     advance(weights)
     finish(wide)
     advance(weights)
-    homes[0].wait()
-    mixed_home = unpack(home_dst[0].reshape(chans, rows), 2.0**17)
+    home.wait()
+    mixed_home = unpack(home_dst[...].reshape(chans, rows), 2.0**17)
     gbuf[zk] = (qt_ref[...] * mixed_home).astype(BF16)
     ring = ring_z(wire, gbuf, x, z, k)
     advance(ring)
@@ -469,10 +470,10 @@
     late.start()
     advance(ring)
     advance(high)
+    advance(ring)
+    advance(high)
     gq_out[...] = (mixed_home.T * total).astype(BF16)
     store(gq_out, gq_hbm)
-    advance(ring)
-    advance(high)
     late.wait()
     grad = unpack(gm_dst[...], 2.0**17)
     ((gr, gi),) = forward([grad], outer, inner, turns)
@@ -481,40 +482,44 @@
         [(gr * fr + gi * fi, gi * fr - gr * fi), (gr * pr + gi * pi, gi * pr - gr * pi)],
         outer_back, inner_back, turns,
     )
-    home_src[1] = pack(back_product, 2.0**8)
-    homes[1].start()
-    home_src[2] = pack(back_taps, 1.0)
-    homes[2].start()
+    pair_src[:, 0:16] = pack(back_product, 2.0**8)
+    pair_src[:, 16:32] = pack(back_taps, 1.0)
+    pair.start()
     finish(ring)
     finish(high)
 
-    def columns_of(half):
-        total = jnp.zeros((chans, 128), F32)
+    def columns_of(half, low, count):
+        total = jnp.zeros((count, 128), F32)
         for a in range(4):
-            left = jnp.concatenate([gbuf[4 * a + j] for j in range(4)], axis=1)
+            left = jnp.concatenate([gbuf[4 * a + j, low : low + count] for j in range(4)], axis=1)
             slots = [lax.rem(4 * half + a + 1 + j, WIDE) for j in range(4)]
             right = jnp.concatenate([tall[slots[j], j] for j in range(4)], axis=0)
             total += dot(left, right)
         return total
 
-    half_src[...] = pack(columns_of(1 - x), 1.0)
-    last = wire.go(
-        half_src, half_dst, {"seq": place(1 - x, z, k)}, wire.group(half_src)
-    )
-    mine = columns_of(x)
+    half_sent = wire.group(half_src)
+    last = []
+    for low in (0, chans // 2):
+        part = pl.ds(low, chans // 2)
+        half_src[part] = pack(columns_of(1 - x, low, chans // 2), 1.0)
+        last.append(
+            wire.go(half_src.at[part], half_dst.at[part], {"seq": place(1 - x, z, k)}, half_sent)
+        )
+    mine = columns_of(x, 0, chans)
 
     def arrived(i, scale):
-        homes[i].wait()
-        return unpack(home_dst[i].reshape(chans, rows), scale).T
-
-    grad_product = arrived(1, 2.0**8)
+        return unpack(pair_dst[:, 16 * i : 16 * i + 16].reshape(chans, rows), scale).T
+
+    pair.wait()
+    grad_product = arrived(0, 2.0**8)
     gk_out[...] = (grad_product * v_ref[...].astype(F32)).astype(BF16)
     store(gk_out, gk_hbm)
     gv_out[...] = (grad_product * k_ref[...].astype(F32)).astype(BF16)
     store(gv_out, gv_hbm)
-    gf_out[...] = arrived(2, 1.0) * env
+    gf_out[...] = arrived(1, 1.0) * env
     store(gf_out, gf_hbm)
-    last.wait_recv()
+    for copy in last:
+        copy.wait_recv()
     gw_out[...] = mine + unpack(half_dst[...], 1.0)
     store(gw_out, gw_hbm)
     for copy in stores:
@@ -574,17 +579,19 @@
             pltpu.VMEM((PARTS, 2 * fine, rows), BF16),
             pltpu.VMEM(piece, BF16),
             pltpu.VMEM(piece, BF16),
-            pltpu.VMEM((3, *piece), BF16),
-            pltpu.VMEM((3, *piece), BF16),
+            pltpu.VMEM(piece, BF16),
+            pltpu.VMEM(piece, BF16),
+            pltpu.VMEM((PARTS, 2 * fine, rows), BF16),
+            pltpu.VMEM((PARTS, 2 * fine, rows), BF16),
             pltpu.VMEM((chans, rows), F32),
             pltpu.VMEM((chans, columns), BF16),
             pltpu.VMEM((chans, columns), BF16),
             pltpu.SemaphoreType.DMA((12,)),
             pltpu.SemaphoreType.DMA((5,)),
             pltpu.SemaphoreType.DMA((6,)),
-            pltpu.SemaphoreType.DMA((70,)),
-            pltpu.SemaphoreType.DMA((5,)),
-            pltpu.SemaphoreType.DMA((5,)),
+            pltpu.SemaphoreType.DMA((71,)),
+            pltpu.SemaphoreType.DMA((4,)),
+            pltpu.SemaphoreType.DMA((4,)),
         ],
         compiler_params=pltpu.CompilerParams(
             collective_id=0, has_side_effects=True, vmem_limit_bytes=63 * 2**20

time: 76.1 us -> 76.2 us (level)
  no operation moved by 1% of the time
where the time goes in v7:
time: 76.2 us; the launch traced here: 76.1 us
  Pallas kernels  75.4 us (99%)
    pallas_call x1, Pallas kernels, on_device(): pl.pallas_call(whole, out_shape=out_shape, in_specs=[anywhere] * 12, out_...  73.4 us
    pallas_call x1, Pallas kernels, on_device(): pl.pallas_call(hand_over, out_shape=out_shape, in_specs=[anywhere] * 5, o...  2.02 us

profile of v7, /device:TPU:1, one launch (start us, length us, event | category | flops | bytes accessed | tf_op | source)
XLA Modules:
  0.0 76.1 jit_solution(14979596053841927457)
XLA Ops:
  0.6 73.4 %whole.1 = (bf16[128,512]{1,0:T(8,128)(2,1)}, bf16[128,512]{1,0:T(8,128)(2,1)}, bf16[128,512]{1,0:T(8,128)(2,1)}, f32[128,512]{1,0:T(8,128)}, f32[512,128]{1,0:T(8,128)}) custom-call(bf16[128,512]{1,0:T(8,128)(2,1)} %q_hbm.1, bf16[128,512]{1,0:T(8,128)(2,1)} %k_hbm.1, bf16[128,512]{1,0:T(8,128)(2,1)} %v_hbm.1, f32[128,512]{1,0:T(8,128)} %f_hbm.1, ...), custom_call_target="tpu_custom_call" | custom-call | tf_op jit(solution)/shard_map/whole/pallas_call | solution.py:559
  74.0 2.0 %hand_over.1 = (bf16[128,512]{1,0:T(8,128)(2,1)}, bf16[128,512]{1,0:T(8,128)(2,1)}, bf16[128,512]{1,0:T(8,128)(2,1)}, f32[128,512]{1,0:T(8,128)}, f32[512,128]{1,0:T(8,128)}) custom-call(bf16[128,512]{1,0:T(8,128)(2,1)} %get-tuple-element.10.refs_0_, bf16[128,512]{1,0:T(8,128)(2,1)} %get-tuple-element.11.refs_1_, ...), custom_call_target="tpu_custom_call" | custom-call | tf_op jit(solution)/shard_map/hand_over/pallas_call | solution.py:604
